TPU v7x, 512 devices: a whole 4x8x8 slice. The times are simulated.
512 devices in a mesh: team: 8 (over y_hi, core), blk: 64 (over z, x, y_lo).
Axes of the slice: x: 4, y: 8 (y_hi: 4, y_lo: 2; y = y_hi * 2 + y_lo), z: 8, core: 2. Of those that a mesh axis runs over, the one named last changes fastest.
Arguments:
- xdata: bfloat16 [2048, 131072], P('team', 'blk'), may hold values from -6 to 6
- omega_tiles: bfloat16 [64, 32, 256, 256], P('blk', 'team'), may hold values from -2 to 3, as said below
- tile_rows: int32 [64, 32], P('blk'), may hold values from 0 to 511, as said below
- tile_cols: int32 [64, 32], P('blk'), may hold values from 0 to 511, as said below
Outputs:
- updated_tiles: bfloat16 [64, 32, 256, 256], P('blk', 'team')
Inputs may be any that keep to these rules, and one draw needn't show every extreme that they name: Each index b of blk owns 8 block-rows, each block-row has one owner, and slots 0 to 7 of b hold its block-rows' diagonal tiles (tile_rows = tile_cols); every other slot of b belongs to one of these block-rows. `tile_cols`: within one owner, no two slots name block-columns c with the same c // 8, so one owner needs at most one panel from each index of blk, and needs exactly 32 of them. `omega_tiles`: the diagonal entries of diagonal tiles lie in 1 to 3.
All inputs are finite; a program needn't handle non-finite values.
Results may differ from a plain program's by a relative error of at most 0.017.
Values may be sent and summed in bfloat16 or wider, within the bound.
A program may use at most 128 MiB of HBM per device.

v0:
```python
import jax
import jax.numpy as jnp
from jax import lax
from jax.sharding import PartitionSpec as P


def body(xdata, omega_tiles, tile_rows, tile_cols):
    team_count = lax.axis_size("team")
    peer_count = lax.axis_size("blk")
    tile_size = omega_tiles.shape[2]
    samples = xdata.shape[0]
    rows_here = xdata.shape[1] // tile_size
    per_team = omega_tiles.shape[1]
    slot_rows = tile_rows[0]
    slot_cols = tile_cols[0]
    gathered = lax.all_gather(omega_tiles, "team", axis=1, tiled=True)[0]
    peer_of = slot_cols // rows_here
    sub_of = slot_cols % rows_here
    picks = (peer_of[:, None] == jnp.arange(peer_count, dtype=jnp.int32)[None, :]).astype(jnp.int32)
    wanted = jnp.sum(picks * sub_of[:, None], axis=0).reshape(peer_count, 1)
    asked = lax.all_to_all(wanted, "blk", split_axis=0, concat_axis=0, tiled=True)
    local_panels = xdata.reshape(samples, rows_here, tile_size)
    outgoing = jnp.take(local_panels, asked[:, 0], axis=1)
    received = lax.all_to_all(outgoing, "blk", split_axis=1, concat_axis=1, tiled=True)
    panels = jnp.take(received, peer_of, axis=1)
    products = jnp.einsum("sab,nsb->san", gathered, panels, preferred_element_type=jnp.float32)
    same_row = (slot_rows[:, None] == slot_rows[None, :]).astype(jnp.float32)
    start = lax.axis_index("team") * per_team
    row_products = jnp.einsum(
        "rs,san->ran", same_row, products, precision=lax.Precision.HIGHEST
    ).astype(jnp.bfloat16)
    partials = jnp.einsum("ran,nrb->rab", row_products, panels, preferred_element_type=jnp.float32)
    summed = lax.psum(partials.astype(jnp.bfloat16), "team").astype(jnp.float32)
    team_share = lax.dynamic_slice_in_dim(summed, start, per_team, 0)
    mine_rows = lax.dynamic_slice_in_dim(slot_rows, start, per_team, 0)
    mine_cols = lax.dynamic_slice_in_dim(slot_cols, start, per_team, 0)
    own_tiles = omega_tiles[0].astype(jnp.float32)
    ident = jnp.eye(tile_size, dtype=jnp.float32)
    diag_mask = (mine_rows == mine_cols)[:, None, None] & (ident[None, :, :] > 0.5)
    inverse = jnp.where(diag_mask, 1.0 / jnp.where(diag_mask, own_tiles, 1.0), 0.0)
    gradient = team_share / (samples * team_count) - inverse
    stepped = own_tiles - 0.5 * gradient
    shrunk = jnp.sign(stepped) * jnp.maximum(jnp.abs(stepped) - 0.05, 0.0)
    return jnp.where(diag_mask, stepped, shrunk).astype(jnp.bfloat16)[None]


def solution(mesh):
    return jax.shard_map(
        body,
        mesh=mesh,
        in_specs=(P("team", "blk"), P("blk", "team", None, None), P("blk", None), P("blk", None)),
        out_specs=P("blk", "team", None, None),
        check_vma=False,
    )
```

profile of v0, /device:TPU:1, one launch (start us, length us, event | category | flops | bytes accessed | tf_op | source)
XLA Modules:
  0.0 413.8 jit_solution(7730347516320278538)
XLA Ops:
  6.5 0.7 compare_and_fusion.1
  7.2 0.7 and_select_fusion.4
  7.9 0.1 select_reduce_fusion
  8.0 0.7 copy.21
  8.7 15.3 %all-to-all-start = ((s32[64,1,1]{2,1,0:T(1,128)}), s32[64,1,1]{2,1,0:T(1,128)S(1)}, u32[]{:S(2)}, u32[]{:S(2)}) async-start(s32[64,1,1]{2,1,0:T(1,128)} %copy.21), calls=%async_computation | async-start | bytes 65536 | tf_op jit(solution)/shard_map/all_to_all | solution.py:21
  24.0 1.5 copy.22
  25.5 0.5 copy.23
  26.1 7.2 %all-to-all-done = s32[64,1,1]{2,1,0:T(1,128)S(1)} async-done(((s32[64,1,1]{2,1,0:T(1,128)}), s32[64,1,1]{2,1,0:T(1,128)S(1)}, u32[]{:S(2)}, u32[]{:S(2)}) %all-to-all-start) | async-done | bytes 288 | tf_op jit(solution)/shard_map/all_to_all | solution.py:21
  33.2 1.2 reduce
  34.5 5.4 %gather_fusion = bf16[64,256,256]{2,1,0:T(8,128)(2,1)} fusion(bf16[256,8,256]{2,0,1:T(8,128)(2,1)S(1)} %copy.23, s32[1024]{0:T(1024)S(1)} %pad_clamp_fusion.1), kind=kCustom, calls=%fused_computation | custom fusion | bytes 16777472 | tf_op jit(solution)/shard_map/jit(_take)/gather | solution.py:23
  39.9 7.5 %select_bitcast_fusion = bf16[256,64,256]{2,0,1:T(8,128)(2,1)} fusion(bf16[64,256,256]{2,1,0:T(8,128)(2,1)} %gather_fusion, pred[64]{0:T(512)(128)(4,1)S(1)} %compare_and_fusion), kind=kLoop, calls=%fused_computation.2 | loop fusion | flops 4194304 | bytes 16777280 | tf_op jit(solution)/shard_map/jit(_take)/select_n | solution.py:23
  47.4 0.0 copy-start.3
  47.4 5.9 %all-to-all-start.1 = ((bf16[256,64,256]{2,0,1:T(8,128)(2,1)}), bf16[256,64,256]{2,0,1:T(8,128)(2,1)}, u32[]{:S(2)}, u32[]{:S(2)}) async-start(bf16[256,64,256]{2,0,1:T(8,128)(2,1)} %select_bitcast_fusion), calls=%async_computation.1 | async-start | bytes 16777216 | tf_op jit(solution)/shard_map/all_to_all | solution.py:24
  53.3 0.0 all-gather.2.cloned.1.call-start
  53.4 0.7 all-gather.2.cloned.1.call-update
  54.0 0.2 all-reduce.2.cloned.1.call-start
  54.3 0.0 copy-done.3
  54.3 186.4 %all-to-all-done.1 = bf16[256,64,256]{2,0,1:T(8,128)(2,1)} async-done(((bf16[256,64,256]{2,0,1:T(8,128)(2,1)}), bf16[256,64,256]{2,0,1:T(8,128)(2,1)}, u32[]{:S(2)}, u32[]{:S(2)}) %all-to-all-start.1) | async-done | bytes 8388640 | tf_op jit(solution)/shard_map/all_to_all | solution.py:24
  240.8 6.1 %gather_fusion.1 = bf16[32,256,256]{2,1,0:T(8,128)(2,1)} fusion(bf16[256,64,256]{2,0,1:T(8,128)(2,1)} %all-to-all-done.1, s32[1024]{0:T(1024)S(1)} %pad_clamp_fusion), kind=kCustom, calls=%fused_computation.1 | custom fusion | bytes 8388736 | tf_op jit(solution)/shard_map/jit(_take)/gather | solution.py:25
  246.9 0.0 all-gather.2.cloned.1.call-done
  246.9 8.0 %fusion.6 = f32[32,256,256]{1,2,0:T(8,128)} fusion(bf16[1,32,256,256]{3,2,0,1:T(8,128)(2,1)} %all-gather.2.cloned.1.call-done, bf16[32,256,256]{2,1,0:T(8,128)(2,1)} %gather_fusion.1, pred[32]{0:T(512)(128)(4,1)S(1)} %get-tuple-element.5), kind=kOutput, calls=%fused_computation.10 | convolution fusion | flops 1075838976 | bytes 16777248 | tf_op jit(solution)/shard_map/sab,nsb->san/dot_general | solution.py:26
  254.9 0.0 copy-start.2
  254.9 10.3 %copy.25 = f32[32,256,256]{2,0,1:T(8,128)} copy(f32[32,256,256]{1,2,0:T(8,128)} %fusion.6) | data formatting | bytes 16777216 | tf_op jit(solution)/shard_map/sab,nsb->san/dot_general | solution.py:26
  265.2 0.0 copy-done.2
  265.2 7.8 %convolution_convert_fusion = bf16[32,256,256]{2,0,1:T(8,128)(2,1)S(1)} fusion(f32[32,256,256]{2,0,1:T(8,128)} %copy.25, s32[32]{0:T(128)S(1)} %bitcast.69), kind=kOutput, calls=%fused_computation.11 | convolution fusion | flops 807404544 | bytes 12583040 | tf_op jit(solution)/shard_map/rs,san->ran/dot_general | solution.py:29
  273.0 0.0 copy-done
  273.0 4.8 %fusion.11 = bf16[32,256,256]{2,1,0:T(8,128)(2,1)} fusion(bf16[32,256,256]{2,0,1:T(8,128)(2,1)S(1)} %convolution_convert_fusion, bf16[32,256,256]{2,1,0:T(8,128)(2,1)S(1)} %copy-done, pred[32]{0:T(512)(128)(4,1)S(1)} %get-tuple-element.5), kind=kOutput, calls=%fused_computation.12 | convolution fusion | flops 1077936128 | bytes 12582944 | tf_op jit(solution)/shard_map/ran,nrb->rab/dot_general | solution.py:32
  277.8 0.0 all-reduce.2.cloned.1.call-update
  277.8 0.1 compare_bitcast_fusion
  278.0 126.2 %all-reduce.2.cloned.1.call-done = bf16[32,256,256]{2,1,0:T(8,128)(2,1)} async-done(((bf16[32,256,256]{2,1,0:T(8,128)(2,1)}), bf16[32,256,256]{2,1,0:T(8,128)(2,1)}) %all-reduce.2.cloned.1.call-update) | async-done | bytes 4194320 | tf_op jit(solution)/shard_map/psum | solution.py:33
  404.1 0.0 copy-done.1
  404.1 2.8 fusion.20
  (8 shorter events, 0.1 us)
Async XLA Ops:
  8.7 24.6 %all-to-all-start = ((s32[64,1,1]{2,1,0:T(1,128)}), s32[64,1,1]{2,1,0:T(1,128)S(1)}, u32[]{:S(2)}, u32[]{:S(2)}) async-start(s32[64,1,1]{2,1,0:T(1,128)} %copy.21), calls=%async_computation | async-start | bytes 65536 | tf_op jit(solution)/shard_map/all_to_all | solution.py:21
  47.4 6.9 %copy-start.3 = (s32[1,32]{1,0:T(1,128)S(1)}, s32[1,32]{1,0:T(1,128)}, u32[]{:S(2)}) copy-start(s32[1,32]{1,0:T(1,128)} %param.7) | copy-start | bytes 388
  47.4 193.3 %all-to-all-start.1 = ((bf16[256,64,256]{2,0,1:T(8,128)(2,1)}), bf16[256,64,256]{2,0,1:T(8,128)(2,1)}, u32[]{:S(2)}, u32[]{:S(2)}) async-start(bf16[256,64,256]{2,0,1:T(8,128)(2,1)} %select_bitcast_fusion), calls=%async_computation.1 | async-start | bytes 16777216 | tf_op jit(solution)/shard_map/all_to_all | solution.py:24
  53.3 193.6 %all-gather.2.cloned.1.call-start = ((), (), s32[]{:S(2)}) async-start(), calls=%async_computation.2 | async-start | bytes 4718592 | tf_op jit(solution)/shard_map/all_gather | solution.py:16
  54.0 350.1 %all-reduce.2.cloned.1.call-start = ((), (), s32[]{:S(2)}) async-start(), calls=%async_computation.3 | async-start | bytes 8388608 | tf_op jit(solution)/shard_map/psum | solution.py:33
  254.9 10.3 %copy-start.2 = (s32[1,32]{1,0:T(1,128)S(1)}, s32[1,32]{1,0:T(1,128)}, u32[]{:S(2)}) copy-start(s32[1,32]{1,0:T(1,128)} %param.6) | copy-start | bytes 388
  265.2 7.8 %copy-start = (bf16[32,256,256]{2,1,0:T(8,128)(2,1)S(1)}, bf16[32,256,256]{2,1,0:T(8,128)(2,1)}, u32[]{:S(2)}) copy-start(bf16[32,256,256]{2,1,0:T(8,128)(2,1)} %gather_fusion.1) | copy-start | bytes 12582916
  277.8 126.3 %copy-start.1 = (bf16[1,4,256,256]{3,2,1,0:T(8,128)(2,1)S(1)}, bf16[1,4,256,256]{3,2,1,0:T(8,128)(2,1)}, u32[]{:S(2)}) copy-start(bf16[1,4,256,256]{3,2,1,0:T(8,128)(2,1)} %param.5) | copy-start | bytes 1572868
Sparse Core Ops, SparseCore 0:
  56.3 74.3 all-gather.1
  278.0 126.1 all-reduce.1
where the time goes:
time: 417 us; the launch traced here: 414 us
  waiting for transfers between devices  321 us (77%)
  local copies, waits for them, and re-layouts  24.6 us (6%)
  starting transfers between devices  21.5 us (5%)
  matrix products  20.6 us (5%)
  between operations  13.5 us (3%)
  other arithmetic  13 us (3%)
    all_to_all x1, waiting for transfers between devices, body(): lax.all_to_all(outgoing, 'blk', split_axis=1, concat_axis=1, tiled=True)  186 us
    psum x1, waiting for transfers between devices, body(): summed = lax.psum(partials.astype(jnp.bfloat16), 'team').astype(jnp.float32)  126 us
    all_to_all x1, starting transfers between devices, body(): lax.all_to_all(wanted, 'blk', split_axis=0, concat_axis=0, tiled=True)  15.3 us
    dot_general x1, local copies, waits for them, and re-layouts, body(): jnp.einsum('sab,nsb->san', gathered, panels, preferred_element_type=jnp.f...  10.3 us
  transfers between devices with their start and end apart: 4, of which 3 were waited for; matrix products, arithmetic and copies ran while one was open for 2% of the time, Pallas kernels for 0%

commit v1 on v0

v1 whole, which is shorter than its diff:
```python
import jax
import jax.numpy as jnp
from jax import lax
from jax.experimental import pallas as pl
from jax.experimental.pallas import tpu as pltpu
from jax.sharding import PartitionSpec as P

MESH = pl.DeviceIdType.MESH
NZ, NX, NH = 8, 4, 4
TILE = 256
SLOTS = 32
CHUNKS = 4
ROWS = TILE // CHUNKS
UNITS = NZ * CHUNKS
LAG_Y = 3
LAG_R = 5
OM_STEP = 12

HERE, Y_XM, Y_X2, Y_XP, Y_ME, XP_OWN, XP_RELAY, XP_PAIR, XM_OWN, XM_PAIR, XM_RELAY, X2_OWN, X2_PAIR = range(13)


def kernel(x_ref, om_ref, rows_v, cols_v, rows_s, cols_s, out_ref,
           zb, stgx, ystg, rec, om, yb, acc, gx, grx, gown, hs, relr, fs, fr, wq, wsm, tsm,
           zs, zsh, zr, ss, ys_r, rp_r, rm_r, ends, wsend, wrecv, oms, omr, ocs, ocr, gs, gr, hss, hsr, fss, fsr, loc):
    t = lax.axis_index("team")
    b = lax.axis_index("blk")
    core, yh = t % 2, t // 2
    z, x, y = b // 8, (b // 2) % 4, b % 2

    def plane(dx, f):
        yy = 1 - y if f else y
        return (t, z * 8 + ((x + dx) % NX) * 2 + yy)

    zp = (t, ((z + 1) % NZ) * 8 + b % 8)
    zm = (t, ((z + NZ - 1) % NZ) * 8 + b % 8)
    xp, xm, yq = plane(1, 0), plane(3, 0), plane(0, 1)
    cq = (yh * 2 + 1 - core, b)
    hp = (((yh + 1) % NH) * 2 + core, b)
    hm = (((yh + 3) % NH) * 2 + core, b)

    def remote(src, dst, ssem, rsem, dev):
        return pltpu.make_async_remote_copy(src_ref=src, dst_ref=dst, send_sem=ssem, recv_sem=rsem,
                                            device_id=dev, device_id_type=MESH)

    loads = [pltpu.make_async_copy(x_ref.at[pl.ds(c * ROWS, ROWS), pl.ds(j * TILE, TILE)], zb.at[0, c, j], loc.at[c, j])
             for c in range(CHUNKS) for j in range(8)]
    for copy in loads:
        copy.start()
    om_load = pltpu.make_async_copy(om_ref.at[0], om.at[0, core], loc.at[CHUNKS, 0])
    om_load.start()

    partners = [zp, zm, cq, hp, hm] + [plane(dx, f) for dx in range(NX) for f in range(2) if dx or f]
    barrier = pltpu.get_barrier_semaphore()
    for dev in partners:
        pl.semaphore_signal(barrier, inc=1, device_id=dev, device_id_type=MESH)

    i0 = lax.broadcasted_iota(jnp.int32, (SLOTS, SLOTS), 0)
    i1 = lax.broadcasted_iota(jnp.int32, (SLOTS, SLOTS), 1)
    eye = i0 == i1
    rb = jnp.broadcast_to(rows_v[...], (SLOTS, SLOTS))
    cb = jnp.broadcast_to(cols_v[...], (SLOTS, SLOTS))
    rc = jnp.broadcast_to(jnp.sum(jnp.where(eye, rb, 0), axis=1, keepdims=True), (SLOTS, SLOTS))
    cc = jnp.sum(jnp.where(eye, cb, 0), axis=1, keepdims=True)
    rank = jnp.sum(jnp.where((rb < rc) | ((rb == rc) & (i1 < i0)), 1, 0), axis=1, keepdims=True)
    order = jnp.sum(jnp.where(rank == i1, i0, 0), axis=0, keepdims=True)
    last = jnp.sum(jnp.where(rc <= rb, 1, 0), axis=0, keepdims=True) - 1
    lane = lax.broadcasted_iota(jnp.int32, (SLOTS, 128), 1)
    ccw = jnp.broadcast_to(cc, (SLOTS, 128))
    wanted = jnp.sum(jnp.where((ccw >> 3) == lane, ccw & 7, 0), axis=0, keepdims=True)
    wq[0] = jnp.broadcast_to(wanted, (8, 128))
    tsm_v = wq.at[8]
    tsm_v[0:1, 0:SLOTS] = order
    tsm_v[1:2, 0:SLOTS] = last

    pl.semaphore_wait(barrier, len(partners))

    def w_copy(dx, f):
        place = dx * 2 + f
        return remote(wq.at[0], wq.at[place], wsend.at[place], wrecv.at[place], plane(dx, f))

    others = [(dx, f) for dx in range(NX) for f in range(2) if dx or f]
    for dx, f in others:
        w_copy(dx, f).start()
    t_copy = pltpu.make_async_copy(wq.at[8], tsm, loc.at[CHUNKS, 1])
    t_copy.start()

    def z_copy(d, k, c):
        if d == 0:
            sem = zs.at[0]
            return remote(zb.at[k - 1, c], zb.at[k, c], sem, zr.at[0, k, c], zp)
        return remote(zb.at[(9 - k) % 8, c], zb.at[8 - k, c], zs.at[1], zr.at[1, k, c], zm)

    def z_half(d, c):
        if d == 0:
            return remote(zb.at[3, c], zb.at[4, c], zsh.at[0], zr.at[0, 4, c], zp)
        return remote(zb.at[5, c], zb.at[4, c], zsh.at[1], zr.at[1, 4, c], zm)

    def rows(c):
        return pl.ds(pl.multiple_of(c * ROWS, ROWS), ROWS)

    def y_copy(k, c):
        return remote(ystg.at[k, c], rec.at[k, pl.ds(Y_XM, 4), rows(c)], ss.at[0], ys_r.at[k, c], yq)

    def own_up(k, c):
        return remote(stgx.at[k, c, pl.ds(0, 2)], rec.at[k, pl.ds(XP_OWN, 2), rows(c)], ss.at[1], rp_r.at[k, c], xp)

    def own_down(k, c):
        return remote(stgx.at[k, c, 2], rec.at[k, XM_OWN, rows(c)], ss.at[2], ends.at[0], xm)

    def pair_up(k, c):
        return remote(rec.at[k, Y_XP, rows(c)], rec.at[k, XP_PAIR, rows(c)], ss.at[3], ends.at[1], xp)

    def pair_down(k, c):
        return remote(rec.at[k, pl.ds(Y_XM, 2), rows(c)], rec.at[k, pl.ds(XM_PAIR, 2), rows(c)], ss.at[4], rm_r.at[k, c], xm)

    def relay_up(k, c):
        return remote(rec.at[k, XP_RELAY, rows(c)], rec.at[k, X2_OWN, rows(c)], ss.at[5], ends.at[2], xp)

    def relay_down(k, c):
        return remote(rec.at[k, XM_RELAY, rows(c)], rec.at[k, X2_PAIR, rows(c)], ss.at[6], ends.at[3], xm)

    def pick(k, c):
        holder = ((z - k + NZ) % NZ) * 8 + x * 2 + y
        for f in range(2):
            for e in range(NX):
                idx = wsm[((NX - e) % NX) * 2 + f, 0, holder]
                got = zb[k, c, 0]
                for j in range(1, 8):
                    got = jnp.where(idx == j, zb[k, c, j], got)
                if f == 1:
                    ystg[k, c, (3, 2, 1, 0)[e]] = got
                elif e == 0:
                    rec[k, HERE, rows(c)] = got
                else:
                    stgx[k, c, e - 1] = got
        y_copy(k, c).start()
        own_up(k, c).start()
        own_down(k, c).start()

    def unit(u):
        v = u - CHUNKS
        p, side = v // 2, v % 2
        d = p // CHUNKS + 1
        k = jnp.where(side == 0, d, 8 - d)
        c = p % CHUNKS
        far = v >= 6 * CHUNKS
        k = jnp.where(far, 4, k)
        c = jnp.where(far, (v - 6 * CHUNKS) // 2 + (CHUNKS // 2) * side, c)
        first = u < CHUNKS
        return jnp.where(first, 0, k), jnp.where(first, u, c), jnp.where(first, 0, d), side

    for c in range(CHUNKS):
        for j in range(8):
            loads[c * 8 + j].wait()
        z_copy(0, 1, c).start()
        z_copy(1, 1, c).start()

    om_load.wait()

    def om_copy(d, what):
        far = hp if d == 0 else hm
        if what == 0:
            return remote(om.at[0, core], om.at[1 if d == 0 else 3, core], oms.at[d], omr.at[d], far)
        half = pl.ds(0 if d == 0 else 2, 2)
        return remote(om.at[1 if d == 0 else 3, core, half], om.at[2, core, half], oms.at[2 + d], omr.at[2 + d], far)

    def om_core(g):
        return remote(om.at[g, core], om.at[g, core], ocs.at[g], ocr.at[g], cq)

    om_copy(0, 0).start()
    om_copy(1, 0).start()
    om_core(0).start()

    for dx, f in others:
        w_copy(dx, f).wait_recv()
    w_load = pltpu.make_async_copy(wq.at[pl.ds(0, 8)], wsm, loc.at[CHUNKS, 2])
    w_load.start()
    w_load.wait()

    for c in range(CHUNKS):
        pick(0, c)

    def y_step(u):
        k, c, _, _ = unit(u)
        y_copy(k, c).wait_recv()
        pair_up(k, c).start()
        pair_down(k, c).start()

    def up_step(u):
        k, c, _, _ = unit(u)
        own_up(k, c).wait_recv()
        relay_up(k, c).start()

    def down_step(u):
        k, c, _, _ = unit(u)
        pair_down(k, c).wait_recv()
        relay_down(k, c).start()

    def z_step(u):
        k, c, d, side = unit(u)

        @pl.when(side == 0)
        def _():
            z_copy(0, d, c).wait_recv()

            @pl.when(d < 3)
            def _():
                z_copy(0, d + 1, c).start()

            @pl.when((d == 3) & (c < CHUNKS // 2))
            def _():
                z_half(0, c).start()

        @pl.when(side == 1)
        def _():
            z_copy(1, d, c).wait_recv()

            @pl.when(d < 3)
            def _():
                z_copy(1, d + 1, c).start()

            @pl.when((d == 3) & (c >= CHUNKS // 2))
            def _():
                z_half(1, c).start()

        pick(k, c)

    def step(u, carry):
        @pl.when(u < UNITS)
        def _():
            z_step(u)

        @pl.when((u >= LAG_Y) & (u < UNITS + LAG_Y))
        def _():
            y_step(u - LAG_Y)
            up_step(u - LAG_Y)

        @pl.when(u >= LAG_R)
        def _():
            down_step(u - LAG_R)

        return carry

    def early(u, carry):
        y_step(u)
        up_step(u)
        return carry

    lax.fori_loop(0, CHUNKS - LAG_Y, early, 0)
    lax.fori_loop(CHUNKS, OM_STEP, step, 0)
    om_copy(0, 0).wait_recv()
    om_copy(0, 1).start()
    om_core(1).start()
    om_copy(1, 0).wait_recv()
    om_copy(1, 1).start()
    om_core(3).start()
    lax.fori_loop(OM_STEP, UNITS + LAG_R, step, 0)
    om_copy(0, 1).wait_recv()
    om_copy(1, 1).wait_recv()
    om_core(2).start()
    t_copy.wait()
    for g in (0, 1, 3, 2):
        om_core(g).wait_recv()
    whole = rec.at[:, HERE]
    for i in range(4):
        pltpu.make_async_copy(whole, whole, ends.at[i]).wait()

    def panel(s):
        h = cols_s[0, s] >> 3
        k = (z - (h >> 3) + NZ) & (NZ - 1)
        dx = (x - ((h >> 1) & 3) + NX) & (NX - 1)
        other = (h & 1) != y
        own = jnp.where(dx == 0, HERE, jnp.where(dx == 1, XP_OWN, jnp.where(dx == 2, X2_OWN, XM_OWN)))
        pair = jnp.where(dx == 0, Y_ME, jnp.where(dx == 1, XP_PAIR, jnp.where(dx == 2, X2_PAIR, XM_PAIR)))
        return rec[k, jnp.where(other, pair, own)]

    def row_step(i, before):
        s = tsm[0, i]
        row = rows_s[0, s]
        who = s >> 2
        tile = om[(yh - (who >> 1) + NH) & (NH - 1), who & 1, s & 3]
        prod = lax.dot_general(tile, panel(s), (((1,), (1,)), ((), ())), preferred_element_type=jnp.float32)
        total = jnp.where(row == before, acc[...], 0.0) + prod
        acc[...] = total
        yb[i] = total.astype(jnp.bfloat16)
        return row

    acc[...] = jnp.zeros_like(acc)
    lax.fori_loop(0, SLOTS, row_step, jnp.int32(-1))

    def grad(g, who, i):
        s = (((yh + g) % NH) * 2 + who) * 4 + i
        return jnp.dot(yb[tsm[1, s]], panel(s), preferred_element_type=jnp.float32)

    def for_pair(g):
        def one(i, carry):
            gx[g, i] = grad(g, 1 - core, i).astype(jnp.bfloat16)
            return carry

        lax.fori_loop(0, 4, one, 0)
        pair_copy(g).start()

    def for_me(g):
        def one(i, carry):
            gown[g, i] = grad(g, core, i)
            return carry

        lax.fori_loop(0, 4, one, 0)

    def pair_copy(g):
        return remote(gx.at[g], grx.at[g], gs.at[g], gr.at[g], cq)

    def half_copy(d):
        half = pl.ds(2 * d, 2)
        return remote(hs.at[half], relr.at[half], hss.at[d], hsr.at[d], hp if d == 0 else hm)

    def last_copy(d, h):
        half = pl.ds(2 * h, 2)
        return remote(fs.at[d, half], fr.at[d, half], fss.at[d, h], fsr.at[d, h], hp if d == 0 else hm)

    for_pair(2)
    for_pair(1)
    for_pair(3)
    for_me(2)
    pair_copy(2).wait_recv()
    hs[...] = (gown[2] + grx[2].astype(jnp.float32)).astype(jnp.bfloat16)
    half_copy(0).start()
    half_copy(1).start()
    for_me(1)
    for_me(3)
    for d, g in ((0, 1), (1, 3)):
        direct = 1 - d
        half = slice(2 * direct, 2 * direct + 2)
        pair_copy(g).wait_recv()
        fs[d, half] = (gown[g, half] + grx[g, half].astype(jnp.float32)).astype(jnp.bfloat16)
        last_copy(d, direct).start()
    for_pair(0)
    for_me(0)
    for d, g in ((0, 1), (1, 3)):
        half = slice(2 * d, 2 * d + 2)
        half_copy(d).wait_recv()
        fs[d, half] = (gown[g, half] + grx[g, half].astype(jnp.float32)
                       + relr[half].astype(jnp.float32)).astype(jnp.bfloat16)
        last_copy(d, d).start()
    pair_copy(0).wait_recv()
    for d in range(2):
        for h in range(2):
            last_copy(d, h).wait_recv()

    e0 = lax.broadcasted_iota(jnp.int32, (TILE, TILE), 0)
    e1 = lax.broadcasted_iota(jnp.int32, (TILE, TILE), 1)
    for i in range(4):
        s = t * 4 + i
        total = (gown[0, i] + grx[0, i].astype(jnp.float32)) + (fr[0, i].astype(jnp.float32) + fr[1, i].astype(jnp.float32))
        own = om[0, core, i].astype(jnp.float32)
        diag = jnp.where(rows_s[0, s] == cols_s[0, s], e0, -1) == e1
        inverse = jnp.where(diag, 1.0 / jnp.where(diag, own, 1.0), 0.0)
        stepped = own - 0.5 * (total / 2048.0 - inverse)
        shrunk = stepped - jnp.clip(stepped, -0.05, 0.05)
        out_ref[0, i] = jnp.where(diag, stepped, shrunk).astype(jnp.bfloat16)

    for dx, f in others:
        w_copy(dx, f).wait_send()
    for d in range(2):
        three = zb.at[pl.ds(0, 3)]
        pltpu.make_async_copy(three, three, zs.at[d]).wait()
        rest = zb.at[3, pl.ds(0, CHUNKS // 2)]
        pltpu.make_async_copy(rest, rest, zsh.at[d]).wait()
        om_copy(d, 0).wait_send()
        om_copy(d, 1).wait_send()
        half_copy(d).wait_send()
        for h in range(2):
            last_copy(d, h).wait_send()
    for g in range(4):
        om_core(g).wait_send()
        pair_copy(g).wait_send()
    for i, n in enumerate((4, 2, 1, 1, 2, 1, 1)):
        sent = rec.at[:, pl.ds(0, n)]
        pltpu.make_async_copy(sent, sent, ss.at[i]).wait()


def body(xdata, omega_tiles, tile_rows, tile_cols):
    bf, f32, i32 = jnp.bfloat16, jnp.float32, jnp.int32
    tile = (TILE, TILE)
    dma = pltpu.SemaphoreType.DMA
    vmem = pl.BlockSpec(memory_space=pltpu.VMEM)
    smem = pl.BlockSpec(memory_space=pltpu.SMEM)
    hbm = pl.BlockSpec(memory_space=pl.ANY)
    return pl.pallas_call(
        kernel,
        out_shape=jax.ShapeDtypeStruct(omega_tiles.shape, bf),
        in_specs=[hbm, hbm, vmem, vmem, smem, smem],
        out_specs=vmem,
        scratch_shapes=[
            pltpu.VMEM((NZ, CHUNKS, 8, ROWS, TILE), bf),
            pltpu.VMEM((NZ, CHUNKS, 3, ROWS, TILE), bf),
            pltpu.VMEM((NZ, CHUNKS, 4, ROWS, TILE), bf),
            pltpu.VMEM((NZ, 13) + tile, bf),
            pltpu.VMEM((NH, 2, 4) + tile, bf),
            pltpu.VMEM((SLOTS,) + tile, bf),
            pltpu.VMEM(tile, f32),
            pltpu.VMEM((NH, 4) + tile, bf),
            pltpu.VMEM((NH, 4) + tile, bf),
            pltpu.VMEM((NH, 4) + tile, f32),
            pltpu.VMEM((4,) + tile, bf),
            pltpu.VMEM((4,) + tile, bf),
            pltpu.VMEM((2, 4) + tile, bf),
            pltpu.VMEM((2, 4) + tile, bf),
            pltpu.VMEM((9, 8, 128), i32),
            pltpu.SMEM((8, 8, 128), i32),
            pltpu.SMEM((8, 128), i32),
            dma((2,)), dma((2,)), dma((2, 5, CHUNKS)),
            dma((7,)), dma((NZ, CHUNKS)), dma((NZ, CHUNKS)), dma((NZ, CHUNKS)), dma((4,)),
            dma((8,)), dma((8,)),
            dma((4,)), dma((4,)), dma((4,)), dma((4,)),
            dma((4,)), dma((4,)), dma((2,)), dma((2,)), dma((2, 2)), dma((2, 2)),
            dma((CHUNKS + 1, 8)),
        ],
        compiler_params=pltpu.CompilerParams(
            collective_id=0, has_side_effects=True, vmem_limit_bytes=60 * 1024 * 1024
        ),
    )(xdata, omega_tiles, tile_rows, tile_cols, tile_rows, tile_cols)


def solution(mesh):
    return jax.shard_map(
        body,
        mesh=mesh,
        in_specs=(P("team", "blk"), P("blk", "team", None, None), P("blk", None), P("blk", None)),
        out_specs=P("blk", "team", None, None),
        check_vma=False,
    )
```

time: 417 us -> 198 us (0.47)
  the two profiles are of different devices: /device:TPU:1 before, /device:TPU:11 now
where the time goes in v1:
time: 198 us
  Pallas kernels  196 us (99%)
    pallas_call x1, Pallas kernels, body(): pl.pallas_call(kernel, out_shape=jax.ShapeDtypeStruct(omega_tiles.shape,...  196 us

profile of v1, /device:TPU:11, one launch (start us, length us, event | category | flops | bytes accessed | tf_op | source)
XLA Modules:
  0.0 198.1 jit_solution(10417576165928188990)
XLA Ops:
  0.0 196.2 %shard_map.46 = bf16[1,4,256,256]{3,2,1,0:T(8,128)(2,1)} custom-call(bf16[256,2048]{1,0:T(8,128)(2,1)} %x_ref.1, bf16[1,4,256,256]{3,2,1,0:T(8,128)(2,1)} %om_ref.1, s32[1,32]{1,0:T(1,128)} %rows_s.1, s32[1,32]{1,0:T(1,128)} %cols_s.1, s32[1,32]{1,0:T(1,128)} %rows_s.1, s32[1,32]{1,0:T(1,128)} %cols_s.1), custom_call_target="tpu_custom_call" | custom-call | tf_op jit(solution)/shard_map/pallas_call | solution.py:389
  196.2 1.9 copy.6

commit v2 on v1

--- a/solution.py
+++ b/solution.py
@@ -11,17 +11,17 @@
 SLOTS = 32
 CHUNKS = 4
 ROWS = TILE // CHUNKS
-UNITS = NZ * CHUNKS
-LAG_Y = 3
-LAG_R = 5
-OM_STEP = 12
-
-HERE, Y_XM, Y_X2, Y_XP, Y_ME, XP_OWN, XP_RELAY, XP_PAIR, XM_OWN, XM_PAIR, XM_RELAY, X2_OWN, X2_PAIR = range(13)
+NEAR = 3
+UNITS = NZ * NEAR
+LAG = 3
+OM_STEP = 10
+
+HERE, Y_XM, Y_X2, Y_XP, Y_ME, XP_OWN, XP_PAIR, XM_OWN, XM_PAIR, X2_OWN, X2_PAIR = range(11)
 
 
 def kernel(x_ref, om_ref, rows_v, cols_v, rows_s, cols_s, out_ref,
-           zb, stgx, ystg, rec, om, yb, acc, gx, grx, gown, hs, relr, fs, fr, wq, wsm, tsm,
-           zs, zsh, zr, ss, ys_r, rp_r, rm_r, ends, wsend, wrecv, oms, omr, ocs, ocr, gs, gr, hss, hsr, fss, fsr, loc):
+           zb, z2, stgx, ystg, rec, om, yb, acc, gx, grx, gown, hs, relr, fs, fr, wq, wsm, tsm,
+           zs, zsh, zr, z2s, z2h, z2r, gys, gyr, ss, ys_r, ends, wsend, wrecv, oms, omr, ocs, ocr, gs, gr, hss, hsr, fss, fsr, loc):
     t = lax.axis_index("team")
     b = lax.axis_index("blk")
     core, yh = t % 2, t // 2
@@ -33,7 +33,7 @@
 
     zp = (t, ((z + 1) % NZ) * 8 + b % 8)
     zm = (t, ((z + NZ - 1) % NZ) * 8 + b % 8)
-    xp, xm, yq = plane(1, 0), plane(3, 0), plane(0, 1)
+    xp, x2, xm, yq = plane(1, 0), plane(2, 0), plane(3, 0), plane(0, 1)
     cq = (yh * 2 + 1 - core, b)
     hp = (((yh + 1) % NH) * 2 + core, b)
     hm = (((yh + 3) % NH) * 2 + core, b)
@@ -42,7 +42,8 @@
         return pltpu.make_async_remote_copy(src_ref=src, dst_ref=dst, send_sem=ssem, recv_sem=rsem,
                                             device_id=dev, device_id_type=MESH)
 
-    loads = [pltpu.make_async_copy(x_ref.at[pl.ds(c * ROWS, ROWS), pl.ds(j * TILE, TILE)], zb.at[0, c, j], loc.at[c, j])
+    loads = [pltpu.make_async_copy(x_ref.at[pl.ds(c * ROWS, ROWS), pl.ds(j * TILE, TILE)], (zb.at[0, c, j] if c < NEAR else z2.at[0, j]),
+                                   loc.at[c, j])
              for c in range(CHUNKS) for j in range(8)]
     for copy in loads:
         copy.start()
@@ -86,8 +87,7 @@
 
     def z_copy(d, k, c):
         if d == 0:
-            sem = zs.at[0]
-            return remote(zb.at[k - 1, c], zb.at[k, c], sem, zr.at[0, k, c], zp)
+            return remote(zb.at[k - 1, c], zb.at[k, c], zs.at[0], zr.at[0, k, c], zp)
         return remote(zb.at[(9 - k) % 8, c], zb.at[8 - k, c], zs.at[1], zr.at[1, k, c], zm)
 
     def z_half(d, c):
@@ -95,61 +95,78 @@
             return remote(zb.at[3, c], zb.at[4, c], zsh.at[0], zr.at[0, 4, c], zp)
         return remote(zb.at[5, c], zb.at[4, c], zsh.at[1], zr.at[1, 4, c], zm)
 
+    def z2_copy(d, k):
+        if d == 0:
+            return remote(z2.at[k - 1], z2.at[k], z2s.at[0], z2r.at[0, k], zp)
+        return remote(z2.at[(9 - k) % 8], z2.at[8 - k], z2s.at[1], z2r.at[1, k], zm)
+
+    z2_half = remote(z2.at[5], z2.at[4], z2h.at[0], z2r.at[1, 4], zm)
+    gather_y = remote(z2.at[0, pl.ds(0, 8)], z2.at[0, pl.ds(8, 8)], gys.at[0], gyr.at[0], yq)
+
     def rows(c):
-        return pl.ds(pl.multiple_of(c * ROWS, ROWS), ROWS)
+        return pl.ds(c * ROWS if isinstance(c, int) else pl.multiple_of(c * ROWS, ROWS), ROWS)
 
     def y_copy(k, c):
         return remote(ystg.at[k, c], rec.at[k, pl.ds(Y_XM, 4), rows(c)], ss.at[0], ys_r.at[k, c], yq)
 
-    def own_up(k, c):
-        return remote(stgx.at[k, c, pl.ds(0, 2)], rec.at[k, pl.ds(XP_OWN, 2), rows(c)], ss.at[1], rp_r.at[k, c], xp)
-
-    def own_down(k, c):
-        return remote(stgx.at[k, c, 2], rec.at[k, XM_OWN, rows(c)], ss.at[2], ends.at[0], xm)
-
-    def pair_up(k, c):
-        return remote(rec.at[k, Y_XP, rows(c)], rec.at[k, XP_PAIR, rows(c)], ss.at[3], ends.at[1], xp)
-
-    def pair_down(k, c):
-        return remote(rec.at[k, pl.ds(Y_XM, 2), rows(c)], rec.at[k, pl.ds(XM_PAIR, 2), rows(c)], ss.at[4], rm_r.at[k, c], xm)
-
-    def relay_up(k, c):
-        return remote(rec.at[k, XP_RELAY, rows(c)], rec.at[k, X2_OWN, rows(c)], ss.at[5], ends.at[2], xp)
-
-    def relay_down(k, c):
-        return remote(rec.at[k, XM_RELAY, rows(c)], rec.at[k, X2_PAIR, rows(c)], ss.at[6], ends.at[3], xm)
+    def send_own(k, c):
+        for i, (place, dev) in enumerate(((XP_OWN, xp), (XM_OWN, xm), (X2_OWN, x2))):
+            remote(stgx.at[k, c, i], rec.at[k, place, rows(c)], ss.at[1 + i], ends.at[i], dev).start()
+
+    def send_pair(k, c):
+        for i, (here, place, dev) in enumerate(((Y_XP, XP_PAIR, xp), (Y_XM, XM_PAIR, xm), (Y_X2, X2_PAIR, x2))):
+            remote(rec.at[k, here, rows(c)], rec.at[k, place, rows(c)], ss.at[4 + i], ends.at[3 + i], dev).start()
+
+    def choose(idx, panels):
+        got = panels(0)
+        for j in range(1, 8):
+            got = jnp.where(idx == j, panels(j), got)
+        return got
+
+    def want(e, f, k, other):
+        holder = ((z - k + NZ) % NZ) * 8 + x * 2 + (1 - y if other else y)
+        return wsm[((NX - e) % NX) * 2 + f, 0, holder]
+
+    def keep_own(k, c, e, got):
+        if e == 0:
+            rec[k, HERE, rows(c)] = got
+        else:
+            stgx[k, c, (0, 2, 1)[e - 1]] = got
 
     def pick(k, c):
-        holder = ((z - k + NZ) % NZ) * 8 + x * 2 + y
-        for f in range(2):
-            for e in range(NX):
-                idx = wsm[((NX - e) % NX) * 2 + f, 0, holder]
-                got = zb[k, c, 0]
-                for j in range(1, 8):
-                    got = jnp.where(idx == j, zb[k, c, j], got)
-                if f == 1:
-                    ystg[k, c, (3, 2, 1, 0)[e]] = got
-                elif e == 0:
-                    rec[k, HERE, rows(c)] = got
-                else:
-                    stgx[k, c, e - 1] = got
+        def panels(j):
+            return zb[k, c, j]
+
+        for e in range(NX):
+            ystg[k, c, (3, 2, 1, 0)[e]] = choose(want(e, 1, k, False), panels)
         y_copy(k, c).start()
-        own_up(k, c).start()
-        own_down(k, c).start()
+        for e in range(NX):
+            keep_own(k, c, e, choose(want(e, 0, k, False), panels))
+        send_own(k, c)
+
+    def pick_whole(k):
+        for e in range(NX):
+            keep_own(k, NEAR, e, choose(want(e, 0, k, False), lambda j: z2[k, j]))
+        send_own(k, NEAR)
+        for e in range(NX):
+            rec[k, (Y_ME, Y_XP, Y_X2, Y_XM)[e], rows(NEAR)] = choose(want(e, 0, k, True), lambda j: z2[k, 8 + j])
+        send_pair(k, NEAR)
 
     def unit(u):
-        v = u - CHUNKS
-        p, side = v // 2, v % 2
-        d = p // CHUNKS + 1
-        k = jnp.where(side == 0, d, 8 - d)
-        c = p % CHUNKS
-        far = v >= 6 * CHUNKS
-        k = jnp.where(far, 4, k)
-        c = jnp.where(far, (v - 6 * CHUNKS) // 2 + (CHUNKS // 2) * side, c)
-        first = u < CHUNKS
-        return jnp.where(first, 0, k), jnp.where(first, u, c), jnp.where(first, 0, d), side
-
-    for c in range(CHUNKS):
+        v = u - NEAR
+        far = v >= 6 * NEAR
+        w = v - 6 * NEAR
+        d = v // (2 * NEAR) + 1
+        side = jnp.where(far, w % 2, v % 2)
+        k = jnp.where(far, 4, jnp.where(side == 0, d, 8 - d))
+        c = jnp.where(far, (2 * w) % 3, (v % (2 * NEAR)) // 2)
+        first = u < NEAR
+        return jnp.where(first, 0, k), jnp.where(first, u, c), d, side
+
+    for j in range(8):
+        loads[NEAR * 8 + j].wait()
+    gather_y.start()
+    for c in range(NEAR):
         for j in range(8):
             loads[c * 8 + j].wait()
         z_copy(0, 1, c).start()
@@ -177,24 +194,18 @@
     w_load.start()
     w_load.wait()
 
-    for c in range(CHUNKS):
+    pick(0, 0)
+    gather_y.wait_recv()
+    z2_copy(0, 1).start()
+    z2_copy(1, 1).start()
+    for c in range(1, NEAR):
         pick(0, c)
+    pick_whole(0)
 
     def y_step(u):
         k, c, _, _ = unit(u)
         y_copy(k, c).wait_recv()
-        pair_up(k, c).start()
-        pair_down(k, c).start()
-
-    def up_step(u):
-        k, c, _, _ = unit(u)
-        own_up(k, c).wait_recv()
-        relay_up(k, c).start()
-
-    def down_step(u):
-        k, c, _, _ = unit(u)
-        pair_down(k, c).wait_recv()
-        relay_down(k, c).start()
+        send_pair(k, c)
 
     def z_step(u):
         k, c, d, side = unit(u)
@@ -207,7 +218,7 @@
             def _():
                 z_copy(0, d + 1, c).start()
 
-            @pl.when((d == 3) & (c < CHUNKS // 2))
+            @pl.when((d == 3) & (c < 2))
             def _():
                 z_half(0, c).start()
 
@@ -219,42 +230,58 @@
             def _():
                 z_copy(1, d + 1, c).start()
 
-            @pl.when((d == 3) & (c >= CHUNKS // 2))
+            @pl.when((d == 3) & (c == 2))
             def _():
                 z_half(1, c).start()
 
         pick(k, c)
 
+    def whole_step(d):
+        z2_copy(0, d).wait_recv()
+
+        @pl.when(d < 3)
+        def _():
+            z2_copy(0, d + 1).start()
+
+        z2_copy(1, d).wait_recv()
+
+        @pl.when(d < 3)
+        def _():
+            z2_copy(1, d + 1).start()
+
+        @pl.when(d == 3)
+        def _():
+            z2_half.start()
+
+        pick_whole(d)
+        pick_whole(8 - d)
+
     def step(u, carry):
         @pl.when(u < UNITS)
         def _():
             z_step(u)
 
-        @pl.when((u >= LAG_Y) & (u < UNITS + LAG_Y))
-        def _():
-            y_step(u - LAG_Y)
-            up_step(u - LAG_Y)
-
-        @pl.when(u >= LAG_R)
-        def _():
-            down_step(u - LAG_R)
+        y_step(u - LAG)
+
+        @pl.when((u < UNITS - 3) & (u % 6 == 2))
+        def _():
+            whole_step((u - NEAR) // 6 + 1)
+
+        @pl.when(u == UNITS - 1)
+        def _():
+            z2_copy(1, 4).wait_recv()
+            pick_whole(4)
 
         return carry
 
-    def early(u, carry):
-        y_step(u)
-        up_step(u)
-        return carry
-
-    lax.fori_loop(0, CHUNKS - LAG_Y, early, 0)
-    lax.fori_loop(CHUNKS, OM_STEP, step, 0)
+    lax.fori_loop(NEAR, OM_STEP, step, 0)
     om_copy(0, 0).wait_recv()
     om_copy(0, 1).start()
     om_core(1).start()
     om_copy(1, 0).wait_recv()
     om_copy(1, 1).start()
     om_core(3).start()
-    lax.fori_loop(OM_STEP, UNITS + LAG_R, step, 0)
+    lax.fori_loop(OM_STEP, UNITS + LAG, step, 0)
     om_copy(0, 1).wait_recv()
     om_copy(1, 1).wait_recv()
     om_core(2).start()
@@ -262,7 +289,7 @@
     for g in (0, 1, 3, 2):
         om_core(g).wait_recv()
     whole = rec.at[:, HERE]
-    for i in range(4):
+    for i in range(6):
         pltpu.make_async_copy(whole, whole, ends.at[i]).wait()
 
     def panel(s):
@@ -361,10 +388,13 @@
 
     for dx, f in others:
         w_copy(dx, f).wait_send()
+    gather_y.wait_send()
+    z2_half.wait_send()
     for d in range(2):
-        three = zb.at[pl.ds(0, 3)]
+        three, three2 = zb.at[pl.ds(0, 3)], z2.at[pl.ds(0, 3)]
         pltpu.make_async_copy(three, three, zs.at[d]).wait()
-        rest = zb.at[3, pl.ds(0, CHUNKS // 2)]
+        pltpu.make_async_copy(three2, three2, z2s.at[d]).wait()
+        rest = zb.at[3, pl.ds(0, 2 - d)]
         pltpu.make_async_copy(rest, rest, zsh.at[d]).wait()
         om_copy(d, 0).wait_send()
         om_copy(d, 1).wait_send()
@@ -374,9 +404,9 @@
     for g in range(4):
         om_core(g).wait_send()
         pair_copy(g).wait_send()
-    for i, n in enumerate((4, 2, 1, 1, 2, 1, 1)):
-        sent = rec.at[:, pl.ds(0, n)]
-        pltpu.make_async_copy(sent, sent, ss.at[i]).wait()
+    pltpu.make_async_copy(ystg, ystg, ss.at[0]).wait()
+    for i in range(6):
+        pltpu.make_async_copy(whole, whole, ss.at[1 + i]).wait()
 
 
 def body(xdata, omega_tiles, tile_rows, tile_cols):
@@ -392,10 +422,11 @@
         in_specs=[hbm, hbm, vmem, vmem, smem, smem],
         out_specs=vmem,
         scratch_shapes=[
-            pltpu.VMEM((NZ, CHUNKS, 8, ROWS, TILE), bf),
+            pltpu.VMEM((NZ, NEAR, 8, ROWS, TILE), bf),
+            pltpu.VMEM((NZ, 16, ROWS, TILE), bf),
             pltpu.VMEM((NZ, CHUNKS, 3, ROWS, TILE), bf),
-            pltpu.VMEM((NZ, CHUNKS, 4, ROWS, TILE), bf),
-            pltpu.VMEM((NZ, 13) + tile, bf),
+            pltpu.VMEM((NZ, NEAR, 4, ROWS, TILE), bf),
+            pltpu.VMEM((NZ, 11) + tile, bf),
             pltpu.VMEM((NH, 2, 4) + tile, bf),
             pltpu.VMEM((SLOTS,) + tile, bf),
             pltpu.VMEM(tile, f32),
@@ -409,8 +440,9 @@
             pltpu.VMEM((9, 8, 128), i32),
             pltpu.SMEM((8, 8, 128), i32),
             pltpu.SMEM((8, 128), i32),
-            dma((2,)), dma((2,)), dma((2, 5, CHUNKS)),
-            dma((7,)), dma((NZ, CHUNKS)), dma((NZ, CHUNKS)), dma((NZ, CHUNKS)), dma((4,)),
+            dma((2,)), dma((2,)), dma((2, 5, NEAR)),
+            dma((2,)), dma((1,)), dma((2, 5)), dma((1,)), dma((1,)),
+            dma((7,)), dma((NZ, NEAR)), dma((6,)),
             dma((8,)), dma((8,)),
             dma((4,)), dma((4,)), dma((4,)), dma((4,)),
             dma((4,)), dma((4,)), dma((2,)), dma((2,)), dma((2, 2)), dma((2, 2)),

time: 198 us -> 188 us (0.949)
  the two profiles are of different devices: /device:TPU:11 before, /device:TPU:9 now
where the time goes in v2:
time: 188 us
  Pallas kernels  186 us (99%)
    pallas_call x1, Pallas kernels, body(): pl.pallas_call(kernel, out_shape=jax.ShapeDtypeStruct(omega_tiles.shape,...  186 us

profile of v2, /device:TPU:9, one launch (start us, length us, event | category | flops | bytes accessed | tf_op | source)
XLA Modules:
  0.0 187.6 jit_solution(6190026980741928223)
XLA Ops:
  0.0 185.7 %shard_map.46 = bf16[1,4,256,256]{3,2,1,0:T(8,128)(2,1)} custom-call(bf16[256,2048]{1,0:T(8,128)(2,1)} %x_ref.1, bf16[1,4,256,256]{3,2,1,0:T(8,128)(2,1)} %om_ref.1, s32[1,32]{1,0:T(1,128)} %rows_s.1, s32[1,32]{1,0:T(1,128)} %cols_s.1, s32[1,32]{1,0:T(1,128)} %rows_s.1, s32[1,32]{1,0:T(1,128)} %cols_s.1), custom_call_target="tpu_custom_call" | custom-call | tf_op jit(solution)/shard_map/pallas_call | solution.py:419
  185.7 1.9 copy.6

commit v3 on v1

v3 whole, which is shorter than its diff:
```python
import jax
import jax.numpy as jnp
from jax import lax
from jax.experimental import pallas as pl
from jax.experimental.pallas import tpu as pltpu
from jax.sharding import PartitionSpec as P

MESH = pl.DeviceIdType.MESH
NZ, NX, NH = 8, 4, 4
TILE = 256
SLOTS = 32
PARTS = (64, 64, 48)
STARTS = (0, 64, 128)
PAIR_START, PAIR_ROWS = 176, 80
OWN, OTHER = 3, 4
OM_STEP = 2


def kernel(x_ref, om_ref, rows_v, cols_v, rows_s, cols_s, out_ref,
           zb0, zb1, zb2, z2, st0, st1, st2, stp, rec, om, yb, acc, gx, grx, gown, hs, relr, fs, fr, wq, wsm, tsm,
           zs, zsh, zr, gys, gyr, near_s, near_r, pair_s, pair_r,
           wsend, wrecv, oms, omr, ocs, ocr, gs, gr, hss, hsr, fss, fsr, loc):
    zb, st = (zb0, zb1, zb2), (st0, st1, st2)
    t = lax.axis_index("team")
    b = lax.axis_index("blk")
    core, yh = t % 2, t // 2
    z, x, y = b // 8, (b // 2) % 4, b % 2

    def plane(dx, f):
        yy = 1 - y if f else y
        return (t, z * 8 + ((x + dx) % NX) * 2 + yy)

    zp = (t, ((z + 1) % NZ) * 8 + b % 8)
    zm = (t, ((z + NZ - 1) % NZ) * 8 + b % 8)
    yq = plane(0, 1)
    cq = (yh * 2 + 1 - core, b)
    hp = (((yh + 1) % NH) * 2 + core, b)
    hm = (((yh + 3) % NH) * 2 + core, b)

    def remote(src, dst, ssem, rsem, dev):
        return pltpu.make_async_remote_copy(src_ref=src, dst_ref=dst, send_sem=ssem, recv_sem=rsem,
                                            device_id=dev, device_id_type=MESH)

    x_loads = []
    for c, (start, size) in enumerate(zip(STARTS + (PAIR_START,), PARTS + (PAIR_ROWS,))):
        x_loads.append([pltpu.make_async_copy(x_ref.at[pl.ds(start, size), pl.ds(j * TILE, TILE)],
                                              (zb[c] if c < OWN else z2).at[0, j], loc.at[c, j]) for j in range(8)])
    for c in (OWN, 0, 1, 2):
        for copy in x_loads[c]:
            copy.start()
    om_load = pltpu.make_async_copy(om_ref.at[0], om.at[0, core], loc.at[4, 0])
    om_load.start()

    partners = [zp, zm, cq, hp, hm] + [plane(dx, f) for dx in range(NX) for f in range(2) if dx or f]
    barrier = pltpu.get_barrier_semaphore()
    for dev in partners:
        pl.semaphore_signal(barrier, inc=1, device_id=dev, device_id_type=MESH)

    i0 = lax.broadcasted_iota(jnp.int32, (SLOTS, SLOTS), 0)
    i1 = lax.broadcasted_iota(jnp.int32, (SLOTS, SLOTS), 1)
    eye = i0 == i1
    rb = jnp.broadcast_to(rows_v[...], (SLOTS, SLOTS))
    cb = jnp.broadcast_to(cols_v[...], (SLOTS, SLOTS))
    rc = jnp.broadcast_to(jnp.sum(jnp.where(eye, rb, 0), axis=1, keepdims=True), (SLOTS, SLOTS))
    cc = jnp.sum(jnp.where(eye, cb, 0), axis=1, keepdims=True)
    rank = jnp.sum(jnp.where((rb < rc) | ((rb == rc) & (i1 < i0)), 1, 0), axis=1, keepdims=True)
    order = jnp.sum(jnp.where(rank == i1, i0, 0), axis=0, keepdims=True)
    last = jnp.sum(jnp.where(rc <= rb, 1, 0), axis=0, keepdims=True) - 1
    lane = lax.broadcasted_iota(jnp.int32, (SLOTS, 128), 1)
    ccw = jnp.broadcast_to(cc, (SLOTS, 128))
    wanted = jnp.sum(jnp.where((ccw >> 3) == lane, ccw & 7, 0), axis=0, keepdims=True)
    wq[0] = jnp.broadcast_to(wanted, (8, 128))
    tsm_v = wq.at[8]
    tsm_v[0:1, 0:SLOTS] = order
    tsm_v[1:2, 0:SLOTS] = last

    pl.semaphore_wait(barrier, len(partners))

    def w_copy(dx, f):
        place = dx * 2 + f
        return remote(wq.at[0], wq.at[place], wsend.at[place], wrecv.at[place], plane(dx, f))

    others = [(dx, f) for dx in range(NX) for f in range(2) if dx or f]
    for dx, f in others:
        w_copy(dx, f).start()
    t_copy = pltpu.make_async_copy(wq.at[8], tsm, loc.at[4, 1])
    t_copy.start()

    def z_ref(u, k):
        if u < OWN:
            return zb[u].at[k]
        return z2.at[k, pl.ds(0 if u == OWN else 8, 8)]

    def z_copy(d, k, u, last=False):
        send = zsh.at[u] if last else zs.at[d, u]
        if d == 0:
            return remote(z_ref(u, k - 1), z_ref(u, k), send, zr.at[0, k, u], zp)
        return remote(z_ref(u, (9 - k) % 8), z_ref(u, 8 - k), send, zr.at[1, k, u], zm)

    def way_of_last(u):
        return 0 if u < OWN else 1

    gather_y = remote(z2.at[0, pl.ds(0, 8)], z2.at[0, pl.ds(8, 8)], gys.at[0], gyr.at[0], yq)

    def choose(e, f, k, other, panels):
        holder = ((z - k + NZ) % NZ) * 8 + x * 2 + (1 - y if other else y)
        idx = wsm[((NX - e) % NX) * 2 + f, 0, holder]
        got = panels(0)
        for j in range(1, 8):
            got = jnp.where(idx == j, panels(j), got)
        return got

    def near_rows(u):
        return pl.ds(STARTS[u], PARTS[u])

    pair_rows = pl.ds(PAIR_START, PAIR_ROWS)

    def near_copy(u, k, i):
        e, f = others[i]
        return remote(st[u].at[k, i], rec.at[k, e, f, near_rows(u)], near_s.at[u, i], near_r.at[u, i], plane(e, f))

    def pair_copies(k, e, half):
        return remote(stp.at[k, half, e - 1], rec.at[k, e, half, pair_rows], pair_s.at[half, e], pair_r.at[half, e], plane(e, 0))

    def pick(u, k):
        if u < OWN:
            for i in (0, 2, 4, 6, 1, 3, 5):
                e, f = others[i]
                st[u][k, i] = choose(e, f, k, False, lambda j: zb[u][k, j])
                near_copy(u, k, i).start()
            rec[k, 0, 0, near_rows(u)] = choose(0, 0, k, False, lambda j: zb[u][k, j])
            return
        half = u - OWN
        for e in (2, 1, 3, 0):
            got = choose(e, 0, k, half == 1, lambda j: z2[k, 8 * half + j])
            if e == 0:
                rec[k, 0, half, pair_rows] = got
            else:
                stp[k, half, e - 1] = got
                pair_copies(k, e, half).start()

    for u in (OWN, 0, 1, 2):
        for copy in x_loads[u]:
            copy.wait()
        if u == OWN:
            gather_y.start()
        z_copy(0, 1, u).start()
        z_copy(1, 1, u).start()

    om_load.wait()

    def om_copy(d, what):
        far = hp if d == 0 else hm
        if what == 0:
            return remote(om.at[0, core], om.at[1 if d == 0 else 3, core], oms.at[d], omr.at[d], far)
        half = pl.ds(0 if d == 0 else 2, 2)
        return remote(om.at[1 if d == 0 else 3, core, half], om.at[2, core, half], oms.at[2 + d], omr.at[2 + d], far)

    def om_core(g):
        return remote(om.at[g, core], om.at[g, core], ocs.at[g], ocr.at[g], cq)

    om_copy(0, 0).start()
    om_copy(1, 0).start()
    om_core(0).start()

    for dx, f in others:
        w_copy(dx, f).wait_recv()
    w_load = pltpu.make_async_copy(wq.at[pl.ds(0, 8)], wsm, loc.at[4, 2])
    w_load.start()
    w_load.wait()

    for u in (OWN, 0, 1, 2):
        pick(u, 0)
    gather_y.wait_recv()
    z_copy(0, 1, OTHER).start()
    z_copy(1, 1, OTHER).start()
    pick(OTHER, 0)

    def step(d, carry):
        for u in (OWN, 0, 1, 2, OTHER):
            for way in range(2):
                z_copy(way, d, u).wait_recv()

                @pl.when(d < 3)
                def _():
                    z_copy(way, d + 1, u).start()

                if way == way_of_last(u):
                    @pl.when(d == 3)
                    def _():
                        z_copy(way, 4, u, True).start()

            pick(u, d)
            pick(u, 8 - d)
        return carry

    lax.fori_loop(1, OM_STEP, step, 0)
    om_copy(0, 0).wait_recv()
    om_copy(0, 1).start()
    om_core(1).start()
    om_copy(1, 0).wait_recv()
    om_copy(1, 1).start()
    om_core(3).start()
    lax.fori_loop(OM_STEP, 4, step, 0)
    for u in (0, OWN, 1, OTHER, 2):
        z_copy(way_of_last(u), 4, u, True).wait_recv()
        pick(u, 4)
    om_copy(0, 1).wait_recv()
    om_copy(1, 1).wait_recv()
    om_core(2).start()
    t_copy.wait()
    for g in (0, 1, 3, 2):
        om_core(g).wait_recv()

    def wait_all(ref, sem):
        pltpu.make_async_copy(ref, ref, sem).wait()

    for u in range(3):
        for i in range(7):
            wait_all(st[u].at[:, 0], near_r.at[u, i])
    for half in range(2):
        for e in range(1, NX):
            wait_all(stp.at[:, 0, 0], pair_r.at[half, e])

    def panel(s):
        h = cols_s[0, s] >> 3
        return rec[(z - (h >> 3) + NZ) & (NZ - 1), (x - ((h >> 1) & 3) + NX) & (NX - 1), (h & 1) ^ y]

    def row_step(i, before):
        s = tsm[0, i]
        row = rows_s[0, s]
        who = s >> 2
        tile = om[(yh - (who >> 1) + NH) & (NH - 1), who & 1, s & 3]
        prod = lax.dot_general(tile, panel(s), (((1,), (1,)), ((), ())), preferred_element_type=jnp.float32)
        total = jnp.where(row == before, acc[...], 0.0) + prod
        acc[...] = total
        yb[i] = total.astype(jnp.bfloat16)
        return row

    acc[...] = jnp.zeros_like(acc)
    lax.fori_loop(0, SLOTS, row_step, jnp.int32(-1), unroll=4)

    def grad(g, who, i):
        s = (((yh + g) % NH) * 2 + who) * 4 + i
        return jnp.dot(yb[tsm[1, s]], panel(s), preferred_element_type=jnp.float32)

    def for_pair(g):
        def one(i, carry):
            gx[g, i] = grad(g, 1 - core, i).astype(jnp.bfloat16)
            return carry

        lax.fori_loop(0, 4, one, 0, unroll=4)
        pair_copy(g).start()

    def for_me(g):
        def one(i, carry):
            gown[g, i] = grad(g, core, i)
            return carry

        lax.fori_loop(0, 4, one, 0, unroll=4)

    def pair_copy(g):
        return remote(gx.at[g], grx.at[g], gs.at[g], gr.at[g], cq)

    def half_copy(d):
        half = pl.ds(2 * d, 2)
        return remote(hs.at[half], relr.at[half], hss.at[d], hsr.at[d], hp if d == 0 else hm)

    def last_copy(d, h):
        half = pl.ds(2 * h, 2)
        return remote(fs.at[d, half], fr.at[d, half], fss.at[d, h], fsr.at[d, h], hp if d == 0 else hm)

    for_pair(2)
    for_pair(1)
    for_pair(3)
    for_me(2)
    pair_copy(2).wait_recv()
    hs[...] = (gown[2] + grx[2].astype(jnp.float32)).astype(jnp.bfloat16)
    half_copy(0).start()
    half_copy(1).start()
    for_me(1)
    for_me(3)
    for d, g in ((0, 1), (1, 3)):
        direct = 1 - d
        half = slice(2 * direct, 2 * direct + 2)
        pair_copy(g).wait_recv()
        fs[d, half] = (gown[g, half] + grx[g, half].astype(jnp.float32)).astype(jnp.bfloat16)
        last_copy(d, direct).start()
    for_pair(0)
    for_me(0)
    for d, g in ((0, 1), (1, 3)):
        half = slice(2 * d, 2 * d + 2)
        half_copy(d).wait_recv()
        fs[d, half] = (gown[g, half] + grx[g, half].astype(jnp.float32)
                       + relr[half].astype(jnp.float32)).astype(jnp.bfloat16)
        last_copy(d, d).start()
    pair_copy(0).wait_recv()
    for d in range(2):
        for h in range(2):
            last_copy(d, h).wait_recv()

    e0 = lax.broadcasted_iota(jnp.int32, (TILE, TILE), 0)
    e1 = lax.broadcasted_iota(jnp.int32, (TILE, TILE), 1)
    for i in range(4):
        s = t * 4 + i
        total = (gown[0, i] + grx[0, i].astype(jnp.float32)) + (fr[0, i].astype(jnp.float32) + fr[1, i].astype(jnp.float32))
        own = om[0, core, i].astype(jnp.float32)
        diag = jnp.where(rows_s[0, s] == cols_s[0, s], e0, -1) == e1
        inverse = jnp.where(diag, 1.0 / jnp.where(diag, own, 1.0), 0.0)
        stepped = own - 0.5 * (total / 2048.0 - inverse)
        shrunk = stepped - jnp.clip(stepped, -0.05, 0.05)
        out_ref[0, i] = jnp.where(diag, stepped, shrunk).astype(jnp.bfloat16)

    for dx, f in others:
        w_copy(dx, f).wait_send()
    gather_y.wait_send()
    for u in range(5):
        z_copy(way_of_last(u), 4, u, True).wait_send()
        for d in range(2):
            wait_all((zb[u] if u < OWN else z2).at[pl.ds(0, 3), pl.ds(0, 8)], zs.at[d, u])
    for d in range(2):
        om_copy(d, 0).wait_send()
        om_copy(d, 1).wait_send()
        half_copy(d).wait_send()
        for h in range(2):
            last_copy(d, h).wait_send()
    for g in range(4):
        om_core(g).wait_send()
        pair_copy(g).wait_send()
    for u in range(3):
        for i in range(7):
            wait_all(st[u].at[:, 0], near_s.at[u, i])
    for half in range(2):
        for e in range(1, NX):
            wait_all(stp.at[:, 0, 0], pair_s.at[half, e])


def body(xdata, omega_tiles, tile_rows, tile_cols):
    bf, f32, i32 = jnp.bfloat16, jnp.float32, jnp.int32
    tile = (TILE, TILE)
    dma = pltpu.SemaphoreType.DMA
    vmem = pl.BlockSpec(memory_space=pltpu.VMEM)
    smem = pl.BlockSpec(memory_space=pltpu.SMEM)
    hbm = pl.BlockSpec(memory_space=pl.ANY)
    return pl.pallas_call(
        kernel,
        out_shape=jax.ShapeDtypeStruct(omega_tiles.shape, bf),
        in_specs=[hbm, hbm, vmem, vmem, smem, smem],
        out_specs=vmem,
        scratch_shapes=[
            *[pltpu.VMEM((NZ, 8, size, TILE), bf) for size in PARTS],
            pltpu.VMEM((NZ, 16, PAIR_ROWS, TILE), bf),
            *[pltpu.VMEM((NZ, 7, size, TILE), bf) for size in PARTS],
            pltpu.VMEM((NZ, 2, 3, PAIR_ROWS, TILE), bf),
            pltpu.VMEM((NZ, NX, 2) + tile, bf),
            pltpu.VMEM((NH, 2, 4) + tile, bf),
            pltpu.VMEM((SLOTS,) + tile, bf),
            pltpu.VMEM(tile, f32),
            pltpu.VMEM((NH, 4) + tile, bf),
            pltpu.VMEM((NH, 4) + tile, bf),
            pltpu.VMEM((NH, 4) + tile, f32),
            pltpu.VMEM((4,) + tile, bf),
            pltpu.VMEM((4,) + tile, bf),
            pltpu.VMEM((2, 4) + tile, bf),
            pltpu.VMEM((2, 4) + tile, bf),
            pltpu.VMEM((9, 8, 128), i32),
            pltpu.SMEM((8, 8, 128), i32),
            pltpu.SMEM((8, 128), i32),
            dma((2, 5)), dma((5,)), dma((2, 5, 5)),
            dma((1,)), dma((1,)),
            dma((3, 7)), dma((3, 7)), dma((2, 4)), dma((2, 4)),
            dma((8,)), dma((8,)),
            dma((4,)), dma((4,)), dma((4,)), dma((4,)),
            dma((4,)), dma((4,)), dma((2,)), dma((2,)), dma((2, 2)), dma((2, 2)),
            dma((5, 8)),
        ],
        compiler_params=pltpu.CompilerParams(
            collective_id=0, has_side_effects=True, vmem_limit_bytes=60 * 1024 * 1024
        ),
    )(xdata, omega_tiles, tile_rows, tile_cols, tile_rows, tile_cols)


def solution(mesh):
    return jax.shard_map(
        body,
        mesh=mesh,
        in_specs=(P("team", "blk"), P("blk", "team", None, None), P("blk", None), P("blk", None)),
        out_specs=P("blk", "team", None, None),
        check_vma=False,
    )
```

time: 198 us -> 173 us (0.87)
  the two profiles are of different devices: /device:TPU:11 before, /device:TPU:1 now
where the time goes in v3:
time: 173 us
  Pallas kernels  171 us (99%)
  local copies, waits for them, and re-layouts  1.87 us (1%)
    pallas_call x1, Pallas kernels, body(): pl.pallas_call(kernel, out_shape=jax.ShapeDtypeStruct(omega_tiles.shape,...  171 us

profile of v3, /device:TPU:1, one launch (start us, length us, event | category | flops | bytes accessed | tf_op | source)
XLA Modules:
  0.0 173.1 jit_solution(16406527257278037505)
XLA Ops:
  0.0 171.2 %shard_map.46 = bf16[1,4,256,256]{3,2,1,0:T(8,128)(2,1)} custom-call(bf16[256,2048]{1,0:T(8,128)(2,1)} %x_ref.1, bf16[1,4,256,256]{3,2,1,0:T(8,128)(2,1)} %om_ref.1, s32[1,32]{1,0:T(1,128)} %rows_s.1, s32[1,32]{1,0:T(1,128)} %cols_s.1, s32[1,32]{1,0:T(1,128)} %rows_s.1, s32[1,32]{1,0:T(1,128)} %cols_s.1), custom_call_target="tpu_custom_call" | custom-call | tf_op jit(solution)/shard_map/pallas_call | solution.py:345
  171.3 1.9 %copy.6 = bf16[1,4,256,256]{3,2,1,0:T(8,128)(2,1)} copy(bf16[1,4,256,256]{3,2,1,0:T(8,128)(2,1)} %shard_map.46) | data formatting | bytes 1048576

commit v4 on v3

--- a/solution.py
+++ b/solution.py
@@ -13,25 +13,23 @@
 STARTS = (0, 64, 128)
 PAIR_START, PAIR_ROWS = 176, 80
 OWN, OTHER = 3, 4
-OM_STEP = 2
 
 
 def kernel(x_ref, om_ref, rows_v, cols_v, rows_s, cols_s, out_ref,
-           zb0, zb1, zb2, z2, st0, st1, st2, stp, rec, om, yb, acc, gx, grx, gown, hs, relr, fs, fr, wq, wsm, tsm,
-           zs, zsh, zr, gys, gyr, near_s, near_r, pair_s, pair_r,
-           wsend, wrecv, oms, omr, ocs, ocr, gs, gr, hss, hsr, fss, fsr, loc):
-    zb, st = (zb0, zb1, zb2), (st0, st1, st2)
+           zb0, zb1, zb2, z2, st0, st1, st2, stp, sn0, sn1, sn2, snp, rec, om, yb, acc, gx, grx, gown, hs, relr, fs, fr, wq, wqn, wsm, wsn, tsm,
+           zs0, zs, zr, gys, gyr, near_s, near_r, pair_s, pair_r,
+           next_s, next_r, wsend, wrecv, wns, wnr, oms, omr, ocs, ocr, gs, gr, hss, hsr, fss, fsr, loc):
+    zb, st, sn = (zb0, zb1, zb2), (st0, st1, st2), (sn0, sn1, sn2)
     t = lax.axis_index("team")
     b = lax.axis_index("blk")
     core, yh = t % 2, t // 2
     z, x, y = b // 8, (b // 2) % 4, b % 2
 
-    def plane(dx, f):
+    def plane(dx, f, dz=0):
         yy = 1 - y if f else y
-        return (t, z * 8 + ((x + dx) % NX) * 2 + yy)
-
-    zp = (t, ((z + 1) % NZ) * 8 + b % 8)
-    zm = (t, ((z + NZ - 1) % NZ) * 8 + b % 8)
+        return (t, ((z + dz) % NZ) * 8 + ((x + dx) % NX) * 2 + yy)
+
+    zp, zm = plane(0, 0, 1), plane(0, 0, NZ - 1)
     yq = plane(0, 1)
     cq = (yh * 2 + 1 - core, b)
     hp = (((yh + 1) % NH) * 2 + core, b)
@@ -91,20 +89,18 @@
             return zb[u].at[k]
         return z2.at[k, pl.ds(0 if u == OWN else 8, 8)]
 
-    def z_copy(d, k, u, last=False):
-        send = zsh.at[u] if last else zs.at[d, u]
+    def z_copy(d, k, u):
+        send = (zs0 if k == 1 else zs).at[d, u]
         if d == 0:
             return remote(z_ref(u, k - 1), z_ref(u, k), send, zr.at[0, k, u], zp)
         return remote(z_ref(u, (9 - k) % 8), z_ref(u, 8 - k), send, zr.at[1, k, u], zm)
 
-    def way_of_last(u):
-        return 0 if u < OWN else 1
-
     gather_y = remote(z2.at[0, pl.ds(0, 8)], z2.at[0, pl.ds(8, 8)], gys.at[0], gyr.at[0], yq)
 
-    def choose(e, f, k, other, panels):
+    def choose(e, f, k, other, panels, way=None):
         holder = ((z - k + NZ) % NZ) * 8 + x * 2 + (1 - y if other else y)
-        idx = wsm[((NX - e) % NX) * 2 + f, 0, holder]
+        place = ((NX - e) % NX) * 2 + f
+        idx = wsm[place, 0, holder] if way is None else wsn[way, place, 0, holder]
         got = panels(0)
         for j in range(1, 8):
             got = jnp.where(idx == j, panels(j), got)
@@ -139,13 +135,34 @@
                 stp[k, half, e - 1] = got
                 pair_copies(k, e, half).start()
 
+    def next_copy(u, k, way, e, f):
+        dev = plane(e, f if u < OWN else 0, 1 if way == 0 else NZ - 1)
+        there = rec.at[k + 1 if way == 0 else k - 1, e, f, near_rows(u) if u < OWN else pair_rows]
+        here = sn[u].at[way, e * 2 + f] if u < OWN else snp.at[way, f, e]
+        return remote(here, there, next_s.at[way, u], next_r.at[way, u], dev)
+
+    def pick_next(u, k, way):
+        for e in (2, 1, 3, 0):
+            if u < OWN:
+                for f in (1, 0):
+                    sn[u][way, e * 2 + f] = choose(e, f, k, False, lambda j: zb[u][k, j], way)
+                    next_copy(u, k, way, e, f).start()
+            else:
+                half = u - OWN
+                snp[way, half, e] = choose(e, 0, k, half == 1, lambda j: z2[k, 8 * half + j], way)
+                next_copy(u, k, way, e, half).start()
+
+    def first_z(u):
+        for way in range(2):
+            z_copy(way, 1, u).start()
+
     for u in (OWN, 0, 1, 2):
         for copy in x_loads[u]:
             copy.wait()
         if u == OWN:
             gather_y.start()
-        z_copy(0, 1, u).start()
-        z_copy(1, 1, u).start()
+        if u != 2:
+            first_z(u)
 
     om_load.wait()
 
@@ -159,52 +176,70 @@
     def om_core(g):
         return remote(om.at[g, core], om.at[g, core], ocs.at[g], ocr.at[g], cq)
 
-    om_copy(0, 0).start()
-    om_copy(1, 0).start()
-    om_core(0).start()
 
     for dx, f in others:
         w_copy(dx, f).wait_recv()
     w_load = pltpu.make_async_copy(wq.at[pl.ds(0, 8)], wsm, loc.at[4, 2])
     w_load.start()
+    table_up = remote(wq.at[pl.ds(0, 8)], wqn.at[1], wns.at[0], wnr.at[1], zp)
+    table_down = remote(wq.at[pl.ds(0, 8)], wqn.at[0], wns.at[1], wnr.at[0], zm)
+    table_up.start()
+    table_down.start()
     w_load.wait()
 
-    for u in (OWN, 0, 1, 2):
+    pick(OWN, 0)
+    for way in range(2):
+        z_copy(way, 1, OWN).wait_send()
+    first_z(2)
+    pick(0, 0)
+    gather_y.wait_recv()
+    for way in range(2):
+        z_copy(way, 1, 0).wait_send()
+    first_z(OTHER)
+    for u in (1, 2, OTHER):
         pick(u, 0)
-    gather_y.wait_recv()
-    z_copy(0, 1, OTHER).start()
-    z_copy(1, 1, OTHER).start()
-    pick(OTHER, 0)
-
-    def step(d, carry):
-        for u in (OWN, 0, 1, 2, OTHER):
-            for way in range(2):
-                z_copy(way, d, u).wait_recv()
-
-                @pl.when(d < 3)
-                def _():
-                    z_copy(way, d + 1, u).start()
-
-                if way == way_of_last(u):
-                    @pl.when(d == 3)
-                    def _():
-                        z_copy(way, 4, u, True).start()
-
-            pick(u, d)
-            pick(u, 8 - d)
-        return carry
-
-    lax.fori_loop(1, OM_STEP, step, 0)
-    om_copy(0, 0).wait_recv()
-    om_copy(0, 1).start()
-    om_core(1).start()
-    om_copy(1, 0).wait_recv()
-    om_copy(1, 1).start()
-    om_core(3).start()
-    lax.fori_loop(OM_STEP, 4, step, 0)
-    for u in (0, OWN, 1, OTHER, 2):
-        z_copy(way_of_last(u), 4, u, True).wait_recv()
-        pick(u, 4)
+
+    for u in (OWN, 0, 1, 2, OTHER):
+        for way in range(2):
+            z_copy(way, 1, u).wait_recv()
+            z_copy(way, 2, u).start()
+        pick(u, 1)
+        pick(u, 7)
+        if u == 0:
+            om_copy(0, 0).start()
+            om_copy(1, 0).start()
+            om_core(0).start()
+
+    table_up.wait_recv()
+    table_down.wait_recv()
+    n_load = pltpu.make_async_copy(wqn, wsn, loc.at[4, 3])
+    n_load.start()
+    n_load.wait()
+
+    for u in (OWN, 0, 1, 2, OTHER):
+        short = 1 if u < OWN else 0
+        for way in range(2):
+            z_copy(way, 2, u).wait_recv()
+            if way != short:
+                z_copy(way, 3, u).start()
+            else:
+                pick_next(u, 2 if way == 0 else 6, way)
+        pick(u, 2)
+        pick(u, 6)
+        if u == 1:
+            om_copy(0, 0).wait_recv()
+            om_copy(0, 1).start()
+            om_core(1).start()
+            om_copy(1, 0).wait_recv()
+            om_copy(1, 1).start()
+            om_core(3).start()
+
+    for u in (OWN, 0, 1, 2, OTHER):
+        way = 0 if u < OWN else 1
+        z_copy(way, 3, u).wait_recv()
+        pick_next(u, 3 if way == 0 else 5, way)
+        pick(u, 3 if way == 0 else 5)
+
     om_copy(0, 1).wait_recv()
     om_copy(1, 1).wait_recv()
     om_core(2).start()
@@ -217,10 +252,13 @@
 
     for u in range(3):
         for i in range(7):
-            wait_all(st[u].at[:, 0], near_r.at[u, i])
+            wait_all(st[u].at[pl.ds(0, 6), 0], near_r.at[u, i])
     for half in range(2):
         for e in range(1, NX):
-            wait_all(stp.at[:, 0, 0], pair_r.at[half, e])
+            wait_all(stp.at[pl.ds(0, 6), 0, 0], pair_r.at[half, e])
+    for way in range(2):
+        for u in range(5):
+            wait_all(sn[u].at[0] if u < OWN else snp.at[0, 0], next_r.at[way, u])
 
     def panel(s):
         h = cols_s[0, s] >> 3
@@ -238,7 +276,7 @@
         return row
 
     acc[...] = jnp.zeros_like(acc)
-    lax.fori_loop(0, SLOTS, row_step, jnp.int32(-1), unroll=4)
+    lax.fori_loop(0, SLOTS, row_step, jnp.int32(-1), unroll=8)
 
     def grad(g, who, i):
         s = (((yh + g) % NH) * 2 + who) * 4 + i
@@ -271,9 +309,9 @@
         return remote(fs.at[d, half], fr.at[d, half], fss.at[d, h], fsr.at[d, h], hp if d == 0 else hm)
 
     for_pair(2)
+    for_me(2)
     for_pair(1)
     for_pair(3)
-    for_me(2)
     pair_copy(2).wait_recv()
     hs[...] = (gown[2] + grx[2].astype(jnp.float32)).astype(jnp.bfloat16)
     half_copy(0).start()
@@ -314,10 +352,15 @@
     for dx, f in others:
         w_copy(dx, f).wait_send()
     gather_y.wait_send()
+    table_up.wait_send()
+    table_down.wait_send()
     for u in range(5):
-        z_copy(way_of_last(u), 4, u, True).wait_send()
-        for d in range(2):
-            wait_all((zb[u] if u < OWN else z2).at[pl.ds(0, 3), pl.ds(0, 8)], zs.at[d, u])
+        blocks = zb[u] if u < OWN else z2
+        for way in range(2):
+            if u in (1, 2, OTHER):
+                z_copy(way, 1, u).wait_send()
+            long = way == (0 if u < OWN else 1)
+            wait_all(blocks.at[pl.ds(0, 2 if long else 1), pl.ds(0, 8)], zs.at[way, u])
     for d in range(2):
         om_copy(d, 0).wait_send()
         om_copy(d, 1).wait_send()
@@ -329,10 +372,13 @@
         pair_copy(g).wait_send()
     for u in range(3):
         for i in range(7):
-            wait_all(st[u].at[:, 0], near_s.at[u, i])
+            wait_all(st[u].at[pl.ds(0, 6), 0], near_s.at[u, i])
     for half in range(2):
         for e in range(1, NX):
-            wait_all(stp.at[:, 0, 0], pair_s.at[half, e])
+            wait_all(stp.at[pl.ds(0, 6), 0, 0], pair_s.at[half, e])
+    for way in range(2):
+        for u in range(5):
+            wait_all(sn[u].at[0] if u < OWN else snp.at[0, 0], next_s.at[way, u])
 
 
 def body(xdata, omega_tiles, tile_rows, tile_cols):
@@ -352,6 +398,8 @@
             pltpu.VMEM((NZ, 16, PAIR_ROWS, TILE), bf),
             *[pltpu.VMEM((NZ, 7, size, TILE), bf) for size in PARTS],
             pltpu.VMEM((NZ, 2, 3, PAIR_ROWS, TILE), bf),
+            *[pltpu.VMEM((2, 8, size, TILE), bf) for size in PARTS],
+            pltpu.VMEM((2, 2, NX, PAIR_ROWS, TILE), bf),
             pltpu.VMEM((NZ, NX, 2) + tile, bf),
             pltpu.VMEM((NH, 2, 4) + tile, bf),
             pltpu.VMEM((SLOTS,) + tile, bf),
@@ -364,12 +412,15 @@
             pltpu.VMEM((2, 4) + tile, bf),
             pltpu.VMEM((2, 4) + tile, bf),
             pltpu.VMEM((9, 8, 128), i32),
+            pltpu.VMEM((2, 8, 8, 128), i32),
             pltpu.SMEM((8, 8, 128), i32),
+            pltpu.SMEM((2, 8, 8, 128), i32),
             pltpu.SMEM((8, 128), i32),
-            dma((2, 5)), dma((5,)), dma((2, 5, 5)),
+            dma((2, 5)), dma((2, 5)), dma((2, 4, 5)),
             dma((1,)), dma((1,)),
             dma((3, 7)), dma((3, 7)), dma((2, 4)), dma((2, 4)),
-            dma((8,)), dma((8,)),
+            dma((2, 5)), dma((2, 5)),
+            dma((8,)), dma((8,)), dma((2,)), dma((2,)),
             dma((4,)), dma((4,)), dma((4,)), dma((4,)),
             dma((4,)), dma((4,)), dma((2,)), dma((2,)), dma((2, 2)), dma((2, 2)),
             dma((5, 8)),

time: 173 us -> 169 us (0.977)
  Pallas kernels: 171 us -> 167 us
    pallas_call x1, Pallas kernels: 171 us -> 167 us  [body(): pl.pallas_call(kernel, out_shape=jax.ShapeDtypeStruct(omega_tiles.shape,...]
where the time goes in v4:
time: 169 us; the launch traced here: 168 us
  Pallas kernels  167 us (99%)
  local copies, waits for them, and re-layouts  1.87 us (1%)
    pallas_call x1, Pallas kernels, body(): pl.pallas_call(kernel, out_shape=jax.ShapeDtypeStruct(omega_tiles.shape,...  167 us

profile of v4, /device:TPU:1, one launch (start us, length us, event | category | flops | bytes accessed | tf_op | source)
XLA Modules:
  0.0 168.4 jit_solution(16604197664778803314)
XLA Ops:
  0.0 166.5 %shard_map.46 = bf16[1,4,256,256]{3,2,1,0:T(8,128)(2,1)} custom-call(bf16[256,2048]{1,0:T(8,128)(2,1)} %x_ref.1, bf16[1,4,256,256]{3,2,1,0:T(8,128)(2,1)} %om_ref.1, s32[1,32]{1,0:T(1,128)} %rows_s.1, s32[1,32]{1,0:T(1,128)} %cols_s.1, s32[1,32]{1,0:T(1,128)} %rows_s.1, s32[1,32]{1,0:T(1,128)} %cols_s.1), custom_call_target="tpu_custom_call" | custom-call | tf_op jit(solution)/shard_map/pallas_call | solution.py:391
  166.6 1.9 %copy.6 = bf16[1,4,256,256]{3,2,1,0:T(8,128)(2,1)} copy(bf16[1,4,256,256]{3,2,1,0:T(8,128)(2,1)} %shard_map.46) | data formatting | bytes 1048576

commit v5 on v4

--- a/solution.py
+++ b/solution.py
@@ -39,14 +39,17 @@
         return pltpu.make_async_remote_copy(src_ref=src, dst_ref=dst, send_sem=ssem, recv_sem=rsem,
                                             device_id=dev, device_id_type=MESH)
 
+    def wait_all(ref, sem):
+        pltpu.make_async_copy(ref, ref, sem).wait()
+
     x_loads = []
     for c, (start, size) in enumerate(zip(STARTS + (PAIR_START,), PARTS + (PAIR_ROWS,))):
         x_loads.append([pltpu.make_async_copy(x_ref.at[pl.ds(start, size), pl.ds(j * TILE, TILE)],
-                                              (zb[c] if c < OWN else z2).at[0, j], loc.at[c, j]) for j in range(8)])
+                                              (zb[c] if c < OWN else z2).at[0, j], loc.at[c]) for j in range(8)])
     for c in (OWN, 0, 1, 2):
         for copy in x_loads[c]:
             copy.start()
-    om_load = pltpu.make_async_copy(om_ref.at[0], om.at[0, core], loc.at[4, 0])
+    om_load = pltpu.make_async_copy(om_ref.at[0], om.at[0, core], loc.at[4])
     om_load.start()
 
     partners = [zp, zm, cq, hp, hm] + [plane(dx, f) for dx in range(NX) for f in range(2) if dx or f]
@@ -76,12 +79,12 @@
 
     def w_copy(dx, f):
         place = dx * 2 + f
-        return remote(wq.at[0], wq.at[place], wsend.at[place], wrecv.at[place], plane(dx, f))
+        return remote(wq.at[0], wq.at[place], wsend.at[0], wrecv.at[0], plane(dx, f))
 
     others = [(dx, f) for dx in range(NX) for f in range(2) if dx or f]
     for dx, f in others:
         w_copy(dx, f).start()
-    t_copy = pltpu.make_async_copy(wq.at[8], tsm, loc.at[4, 1])
+    t_copy = pltpu.make_async_copy(wq.at[8], tsm, loc.at[5])
     t_copy.start()
 
     def z_ref(u, k):
@@ -92,8 +95,8 @@
     def z_copy(d, k, u):
         send = (zs0 if k == 1 else zs).at[d, u]
         if d == 0:
-            return remote(z_ref(u, k - 1), z_ref(u, k), send, zr.at[0, k, u], zp)
-        return remote(z_ref(u, (9 - k) % 8), z_ref(u, 8 - k), send, zr.at[1, k, u], zm)
+            return remote(z_ref(u, k - 1), z_ref(u, k), send, zr.at[0, k - 1, u], zp)
+        return remote(z_ref(u, (9 - k) % 8), z_ref(u, 8 - k), send, zr.at[1, k - 1, u], zm)
 
     gather_y = remote(z2.at[0, pl.ds(0, 8)], z2.at[0, pl.ds(8, 8)], gys.at[0], gyr.at[0], yq)
 
@@ -113,10 +116,10 @@
 
     def near_copy(u, k, i):
         e, f = others[i]
-        return remote(st[u].at[k, i], rec.at[k, e, f, near_rows(u)], near_s.at[u, i], near_r.at[u, i], plane(e, f))
+        return remote(st[u].at[k, i], rec.at[k, e, f, near_rows(u)], near_s.at[u], near_r.at[u], plane(e, f))
 
     def pair_copies(k, e, half):
-        return remote(stp.at[k, half, e - 1], rec.at[k, e, half, pair_rows], pair_s.at[half, e], pair_r.at[half, e], plane(e, 0))
+        return remote(stp.at[k, half, e - 1], rec.at[k, e, half, pair_rows], pair_s.at[half], pair_r.at[half], plane(e, 0))
 
     def pick(u, k):
         if u < OWN:
@@ -139,7 +142,7 @@
         dev = plane(e, f if u < OWN else 0, 1 if way == 0 else NZ - 1)
         there = rec.at[k + 1 if way == 0 else k - 1, e, f, near_rows(u) if u < OWN else pair_rows]
         here = sn[u].at[way, e * 2 + f] if u < OWN else snp.at[way, f, e]
-        return remote(here, there, next_s.at[way, u], next_r.at[way, u], dev)
+        return remote(here, there, next_s.at[u], next_r.at[u], dev)
 
     def pick_next(u, k, way):
         for e in (2, 1, 3, 0):
@@ -157,11 +160,10 @@
             z_copy(way, 1, u).start()
 
     for u in (OWN, 0, 1, 2):
-        for copy in x_loads[u]:
-            copy.wait()
+        wait_all(z_ref(u, 0), loc.at[u])
         if u == OWN:
             gather_y.start()
-        if u != 2:
+        elif u != 2:
             first_z(u)
 
     om_load.wait()
@@ -177,9 +179,8 @@
         return remote(om.at[g, core], om.at[g, core], ocs.at[g], ocr.at[g], cq)
 
 
-    for dx, f in others:
-        w_copy(dx, f).wait_recv()
-    w_load = pltpu.make_async_copy(wq.at[pl.ds(0, 8)], wsm, loc.at[4, 2])
+    wait_all(wq.at[pl.ds(1, 7)], wrecv.at[0])
+    w_load = pltpu.make_async_copy(wq.at[pl.ds(0, 8)], wsm, loc.at[6])
     w_load.start()
     table_up = remote(wq.at[pl.ds(0, 8)], wqn.at[1], wns.at[0], wnr.at[1], zp)
     table_down = remote(wq.at[pl.ds(0, 8)], wqn.at[0], wns.at[1], wnr.at[0], zm)
@@ -187,36 +188,37 @@
     table_down.start()
     w_load.wait()
 
-    pick(OWN, 0)
-    for way in range(2):
-        z_copy(way, 1, OWN).wait_send()
-    first_z(2)
     pick(0, 0)
-    gather_y.wait_recv()
     for way in range(2):
         z_copy(way, 1, 0).wait_send()
+    first_z(2)
+    pick(1, 0)
+    for way in range(2):
+        z_copy(way, 1, 1).wait_send()
+    first_z(OWN)
+    pick(2, 0)
+    gather_y.wait_recv()
     first_z(OTHER)
-    for u in (1, 2, OTHER):
-        pick(u, 0)
-
-    for u in (OWN, 0, 1, 2, OTHER):
+    om_copy(0, 0).start()
+    om_copy(1, 0).start()
+    om_core(0).start()
+    pick(OWN, 0)
+    pick(OTHER, 0)
+
+    for u in (0, 1, 2, OWN, OTHER):
         for way in range(2):
             z_copy(way, 1, u).wait_recv()
             z_copy(way, 2, u).start()
         pick(u, 1)
         pick(u, 7)
-        if u == 0:
-            om_copy(0, 0).start()
-            om_copy(1, 0).start()
-            om_core(0).start()
 
     table_up.wait_recv()
     table_down.wait_recv()
-    n_load = pltpu.make_async_copy(wqn, wsn, loc.at[4, 3])
+    n_load = pltpu.make_async_copy(wqn, wsn, loc.at[7])
     n_load.start()
     n_load.wait()
 
-    for u in (OWN, 0, 1, 2, OTHER):
+    for u in (0, 1, 2, OWN, OTHER):
         short = 1 if u < OWN else 0
         for way in range(2):
             z_copy(way, 2, u).wait_recv()
@@ -234,7 +236,7 @@
             om_copy(1, 1).start()
             om_core(3).start()
 
-    for u in (OWN, 0, 1, 2, OTHER):
+    for u in (0, 1, 2, OWN, OTHER):
         way = 0 if u < OWN else 1
         z_copy(way, 3, u).wait_recv()
         pick_next(u, 3 if way == 0 else 5, way)
@@ -247,18 +249,12 @@
     for g in (0, 1, 3, 2):
         om_core(g).wait_recv()
 
-    def wait_all(ref, sem):
-        pltpu.make_async_copy(ref, ref, sem).wait()
-
     for u in range(3):
-        for i in range(7):
-            wait_all(st[u].at[pl.ds(0, 6), 0], near_r.at[u, i])
+        wait_all(st[u].at[pl.ds(0, 6)], near_r.at[u])
     for half in range(2):
-        for e in range(1, NX):
-            wait_all(stp.at[pl.ds(0, 6), 0, 0], pair_r.at[half, e])
-    for way in range(2):
-        for u in range(5):
-            wait_all(sn[u].at[0] if u < OWN else snp.at[0, 0], next_r.at[way, u])
+        wait_all(stp.at[pl.ds(0, 6), half], pair_r.at[half])
+    for u in range(5):
+        wait_all(sn[u] if u < OWN else snp.at[:, u - OWN], next_r.at[u])
 
     def panel(s):
         h = cols_s[0, s] >> 3
@@ -349,15 +345,14 @@
         shrunk = stepped - jnp.clip(stepped, -0.05, 0.05)
         out_ref[0, i] = jnp.where(diag, stepped, shrunk).astype(jnp.bfloat16)
 
-    for dx, f in others:
-        w_copy(dx, f).wait_send()
+    wait_all(wq.at[pl.ds(1, 7)], wsend.at[0])
     gather_y.wait_send()
     table_up.wait_send()
     table_down.wait_send()
     for u in range(5):
         blocks = zb[u] if u < OWN else z2
         for way in range(2):
-            if u in (1, 2, OTHER):
+            if u in (2, OWN, OTHER):
                 z_copy(way, 1, u).wait_send()
             long = way == (0 if u < OWN else 1)
             wait_all(blocks.at[pl.ds(0, 2 if long else 1), pl.ds(0, 8)], zs.at[way, u])
@@ -371,14 +366,11 @@
         om_core(g).wait_send()
         pair_copy(g).wait_send()
     for u in range(3):
-        for i in range(7):
-            wait_all(st[u].at[pl.ds(0, 6), 0], near_s.at[u, i])
+        wait_all(st[u].at[pl.ds(0, 6)], near_s.at[u])
     for half in range(2):
-        for e in range(1, NX):
-            wait_all(stp.at[pl.ds(0, 6), 0, 0], pair_s.at[half, e])
-    for way in range(2):
-        for u in range(5):
-            wait_all(sn[u].at[0] if u < OWN else snp.at[0, 0], next_s.at[way, u])
+        wait_all(stp.at[pl.ds(0, 6), half], pair_s.at[half])
+    for u in range(5):
+        wait_all(sn[u] if u < OWN else snp.at[:, u - OWN], next_s.at[u])
 
 
 def body(xdata, omega_tiles, tile_rows, tile_cols):
@@ -416,14 +408,14 @@
             pltpu.SMEM((8, 8, 128), i32),
             pltpu.SMEM((2, 8, 8, 128), i32),
             pltpu.SMEM((8, 128), i32),
-            dma((2, 5)), dma((2, 5)), dma((2, 4, 5)),
+            dma((2, 5)), dma((2, 5)), dma((2, 3, 5)),
             dma((1,)), dma((1,)),
-            dma((3, 7)), dma((3, 7)), dma((2, 4)), dma((2, 4)),
-            dma((2, 5)), dma((2, 5)),
-            dma((8,)), dma((8,)), dma((2,)), dma((2,)),
+            dma((3,)), dma((3,)), dma((2,)), dma((2,)),
+            dma((5,)), dma((5,)),
+            dma((1,)), dma((1,)), dma((2,)), dma((2,)),
             dma((4,)), dma((4,)), dma((4,)), dma((4,)),
             dma((4,)), dma((4,)), dma((2,)), dma((2,)), dma((2, 2)), dma((2, 2)),
-            dma((5, 8)),
+            dma((8,)),
         ],
         compiler_params=pltpu.CompilerParams(
             collective_id=0, has_side_effects=True, vmem_limit_bytes=60 * 1024 * 1024

time: 169 us -> 167 us (0.988)
  the two profiles are of different devices: /device:TPU:1 before, /device:TPU:9 now
where the time goes in v5:
time: 167 us
  Pallas kernels  165 us (99%)
  local copies, waits for them, and re-layouts  1.87 us (1%)
    pallas_call x1, Pallas kernels, body(): pl.pallas_call(kernel, out_shape=jax.ShapeDtypeStruct(omega_tiles.shape,...  165 us

profile of v5, /device:TPU:9, one launch (start us, length us, event | category | flops | bytes accessed | tf_op | source)
XLA Modules:
  0.0 166.8 jit_solution(7851376665095413757)
XLA Ops:
  0.0 164.9 %shard_map.46 = bf16[1,4,256,256]{3,2,1,0:T(8,128)(2,1)} custom-call(bf16[256,2048]{1,0:T(8,128)(2,1)} %x_ref.1, bf16[1,4,256,256]{3,2,1,0:T(8,128)(2,1)} %om_ref.1, s32[1,32]{1,0:T(1,128)} %rows_s.1, s32[1,32]{1,0:T(1,128)} %cols_s.1, s32[1,32]{1,0:T(1,128)} %rows_s.1, s32[1,32]{1,0:T(1,128)} %cols_s.1), custom_call_target="tpu_custom_call" | custom-call | tf_op jit(solution)/shard_map/pallas_call | solution.py:383
  164.9 1.9 %copy.6 = bf16[1,4,256,256]{3,2,1,0:T(8,128)(2,1)} copy(bf16[1,4,256,256]{3,2,1,0:T(8,128)(2,1)} %shard_map.46) | data formatting | bytes 1048576
